TPU v7x, 32 devices: a whole 2x2x4 slice. The times are simulated.
32 devices in a mesh: rep: 8 (over z, core), shard: 4 (over y, x).
Axes of the slice: x: 2, y: 2, z: 4, core: 2. Of those that a mesh axis runs over, the one named last changes fastest.
Arguments:
- hidden_in: bfloat16 [12288, 2048], P(('rep', 'shard')), may hold values from -6 to 6
- segment_ids: int32 [12288], P(('rep', 'shard')), may hold values from 0 to 3, as said below
- attn_norm: bfloat16 [2048], P('shard'), may hold values from 0.5 to 1.5
- attn_router: bfloat16 [2048, 2], P('shard'), may hold values from -0.09375 to 0.09375
- kv_weight: bfloat16 [2048, 4096], P('shard'), may hold values from -0.125 to 0.125
- query_weight: bfloat16 [2, 2048, 2048], P(None, 'shard'), may hold values from -0.125 to 0.125
- out_weight: bfloat16 [2, 2048, 2048], P(None, 'shard'), may hold values from -1 to 1
- mlp_norm: bfloat16 [2048], P('shard'), may hold values from 0.5 to 1.5
- mlp_router: bfloat16 [2048, 2], P('shard'), may hold values from -0.09375 to 0.09375
- gate_weight: bfloat16 [2, 2048, 5632], P(None, None, 'shard'), may hold values from -0.125 to 0.125
- up_weight: bfloat16 [2, 2048, 5632], P(None, None, 'shard'), may hold values from -0.125 to 0.125
- down_weight: bfloat16 [2, 5632, 2048], P(None, 'shard'), may hold values from -0.078125 to 0.078125
- cotangent: bfloat16 [12288, 2048], P(('rep', 'shard')), may hold values from -6 to 6
Outputs:
- output: bfloat16 [12288, 2048], P(('rep', 'shard'))
- input_grad: float32 [12288, 2048], P(('rep', 'shard'))
- attn_norm_grad: float32 [2048], P('shard')
- attn_router_grad: float32 [2048, 2], P('shard')
- kv_weight_grad: float32 [2048, 4096], P('shard')
- query_weight_grad: float32 [2, 2048, 2048], P(None, 'shard')
- out_weight_grad: float32 [2, 2048, 2048], P(None, 'shard')
- mlp_norm_grad: float32 [2048], P('shard')
- mlp_router_grad: float32 [2048, 2], P('shard')
- gate_weight_grad: float32 [2, 2048, 5632], P(None, None, ('shard', 'rep'))
- up_weight_grad: float32 [2, 2048, 5632], P(None, None, ('shard', 'rep'))
- down_weight_grad: float32 [2, 5632, 2048], P(None, ('shard', 'rep'))
Inputs may be any that keep to these rules, and one draw needn't show every extreme that they name: `segment_ids`: within each sequence of 1536 rows the segment numbers never fall and begin at 0.
All inputs are finite; a program needn't handle non-finite values.
Results may differ from a plain program's by a relative error of at most 0.02.
Values may be sent and summed in bfloat16 or wider, within the bound.
No kernel may reach another device: no remote copies, remote signals or barrier semaphores. Data moves between devices by JAX's collectives and lax.ppermute only.
A program may use at most 576 MiB of HBM per device.

v0:
```python
import jax
import jax.numpy as jnp
from jax import lax
from jax.sharding import PartitionSpec as P

HEAD = 128
WIN = 1024


EPSILON = 1e-06
THETA = 10000.0
HIGHEST = lax.Precision.HIGHEST


def from_behind(value, axis, steps):
    count = lax.axis_size(axis)
    initial, last = (max(0, -steps), min(count, count - steps))
    return lax.ppermute(value, axis, [(source, source + steps) for source in range(initial, last)])


def angle_tables(position, half_width):
    frequency = THETA ** (-jnp.arange(half_width, dtype=jnp.float32) / half_width)
    angle = position.astype(jnp.float32)[:, None] * frequency[None, :]
    return (jnp.cos(angle)[:, None, :], jnp.sin(angle)[:, None, :])


def rotate(field, cos_table, sin_table, direction):
    half_width = field.shape[-1] // 2
    first_half = field[..., :half_width]
    second_half = field[..., half_width:]
    return jnp.concatenate(
        [
            first_half * cos_table - direction * (second_half * sin_table),
            second_half * cos_table + direction * (first_half * sin_table),
        ],
        -1,
    )


def norm_back(d_normed, hidden, inv_scale, gain):
    scaled_grad = d_normed * gain
    d_gain = jnp.sum(d_normed * hidden * inv_scale, 0)
    d_hidden = inv_scale * scaled_grad - hidden * inv_scale**3 * jnp.mean(
        scaled_grad * hidden, -1, keepdims=True
    )
    return (d_hidden, d_gain)


def router_back(d_gates, gates, normed, router):
    d_logits = gates * (d_gates - jnp.sum(gates * d_gates, -1, keepdims=True))
    d_router = jnp.dot(normed.astype(jnp.float32).T, d_logits, precision=HIGHEST)
    d_normed = jnp.dot(d_logits, router.astype(jnp.float32).T, precision=HIGHEST)
    return (d_normed, d_router)


def swiglu_back(d_inner, gate_pre, up_pre):
    sigmoid_gate = jax.nn.sigmoid(gate_pre)
    d_gate_pre = (d_inner * up_pre * sigmoid_gate * (1.0 + gate_pre * (1.0 - sigmoid_gate))).astype(
        jnp.bfloat16
    )
    d_up_pre = (d_inner * gate_pre * sigmoid_gate).astype(jnp.bfloat16)
    return (d_gate_pre, d_up_pre)


def on_device(
    hidden_in,
    segment_ids,
    attn_norm,
    attn_router,
    kv_weight,
    query_weight,
    out_weight,
    mlp_norm,
    mlp_router,
    gate_weight,
    up_weight,
    down_weight,
    cotangent,
):
    row_count = hidden_in.shape[0]
    shard_count = lax.axis_size("shard")
    shard_at = lax.axis_index("shard")
    position = shard_at * row_count + jnp.arange(row_count, dtype=jnp.int32)
    cos_table, sin_table = angle_tables(position, HEAD // 2)
    reach_back = min((WIN + row_count - 2) // row_count, shard_count - 1)
    score_scale = HEAD ** (-0.5)

    def fetch_layer():
        return (
            lax.all_gather(attn_norm, "shard", axis=0, tiled=True),
            lax.all_gather(attn_router, "shard", axis=0, tiled=True),
            lax.all_gather(kv_weight, "shard", axis=0, tiled=True),
            lax.all_gather(query_weight, "shard", axis=1, tiled=True),
            lax.all_gather(out_weight, "shard", axis=1, tiled=True),
            lax.all_gather(mlp_norm, "shard", axis=0, tiled=True),
            lax.all_gather(mlp_router, "shard", axis=0, tiled=True),
        )

    norm_one, router_one, kv_full, query_full, out_full, norm_two, router_two = fetch_layer()
    hidden = hidden_in.astype(jnp.float32)
    scale_one = lax.rsqrt(jnp.mean(hidden * hidden, -1, keepdims=True) + EPSILON)
    normed = (hidden * scale_one * norm_one.astype(jnp.float32)).astype(jnp.bfloat16)
    gate_one = jax.nn.softmax(jnp.dot(normed, router_one, preferred_element_type=jnp.float32), -1)
    keyval = jnp.dot(normed, kv_full, preferred_element_type=jnp.float32)
    kv_width = keyval.shape[1] // 2
    head_count = kv_width // HEAD
    own_keys = rotate(
        keyval[:, :kv_width].reshape(row_count, head_count, HEAD), cos_table, sin_table, 1.0
    ).astype(jnp.bfloat16)
    own_values = keyval[:, kv_width:].reshape(row_count, head_count, HEAD).astype(jnp.bfloat16)
    att_experts = query_full.shape[0]
    queries = jnp.einsum("td,edf->etf", normed, query_full, preferred_element_type=jnp.float32)
    queries = rotate(
        queries.reshape(att_experts, row_count, head_count, HEAD), cos_table, sin_table, 1.0
    ).astype(jnp.bfloat16)
    seq_segments = lax.all_gather(segment_ids, "shard", axis=0, tiled=True)
    key_list = [own_keys]
    value_list = [own_values]
    segment_list = [segment_ids]
    place_list = [position]
    for offset in range(1, reach_back + 1):
        far_keys, far_values = from_behind((own_keys, own_values), "shard", offset)
        far_start = jnp.maximum(shard_at - offset, 0) * row_count
        key_list.insert(0, far_keys)
        value_list.insert(0, far_values)
        segment_list.insert(0, lax.dynamic_slice_in_dim(seq_segments, far_start, row_count))
        place_list.insert(0, position - offset * row_count)
    all_keys = jnp.concatenate(key_list, 0)
    all_values = jnp.concatenate(value_list, 0)
    key_segment = jnp.concatenate(segment_list, 0)
    key_place = jnp.concatenate(place_list, 0)
    distance = position[:, None] - key_place[None, :]
    allowed = (
        (segment_ids[:, None] == key_segment[None, :])
        & (distance >= 0)
        & (distance < WIN)
        & (key_place[None, :] >= 0)
    )

    def masked_scores(query_rows):
        raw = (
            jnp.einsum("qhd,khd->hqk", query_rows, all_keys, preferred_element_type=jnp.float32)
            * score_scale
        )
        return jnp.where(allowed[None], raw, -1e30)

    heads_list = []
    row_stats = []
    branch_list = []
    for expert in range(att_experts):
        scores = masked_scores(queries[expert])
        row_top = jnp.max(scores, -1, keepdims=True)
        weights = jnp.exp(scores - row_top)
        row_total = jnp.sum(weights, -1, keepdims=True)
        prob_low = (weights / row_total).astype(jnp.bfloat16)
        heads_out = (
            jnp.einsum("hqk,khd->qhd", prob_low, all_values, preferred_element_type=jnp.float32)
            .reshape(row_count, kv_width)
            .astype(jnp.bfloat16)
        )
        branch = jnp.dot(heads_out, out_full[expert], preferred_element_type=jnp.float32)
        weighted = gate_one[:, expert : expert + 1] * branch
        attn_mix = weighted if expert == 0 else attn_mix + weighted
        heads_list.append(heads_out)
        row_stats.append((row_top, row_total))
        branch_list.append(branch)
    middle = hidden + attn_mix
    scale_two = lax.rsqrt(jnp.mean(middle * middle, -1, keepdims=True) + EPSILON)
    normed_two = (middle * scale_two * norm_two.astype(jnp.float32)).astype(jnp.bfloat16)
    gate_two = jax.nn.softmax(
        jnp.dot(normed_two, router_two, preferred_element_type=jnp.float32), -1
    )
    mlp_experts = gate_weight.shape[0]
    saved_mlp = []
    wide_normed, wide_cot = (
        lax.all_gather(normed_two, "shard", axis=0, tiled=True),
        lax.all_gather(cotangent, "shard", axis=0, tiled=True),
    )
    wide_gate = jax.nn.softmax(
        jnp.dot(wide_normed, router_two, preferred_element_type=jnp.float32), -1
    )
    for expert in range(mlp_experts):
        gate_pre = jnp.dot(wide_normed, gate_weight[expert], preferred_element_type=jnp.float32)
        up_pre = jnp.dot(wide_normed, up_weight[expert], preferred_element_type=jnp.float32)
        inner_act = (jax.nn.silu(gate_pre) * up_pre).astype(jnp.bfloat16)
        expert_out = jnp.dot(inner_act, down_weight[expert], preferred_element_type=jnp.float32)
        weighted = wide_gate[:, expert : expert + 1] * expert_out
        partial_mix = weighted if expert == 0 else partial_mix + weighted
        saved_mlp.append((gate_pre, up_pre, inner_act, expert_out))
    mlp_mix = lax.psum_scatter(
        partial_mix.astype(jnp.bfloat16), "shard", scatter_dimension=0, tiled=True
    ).astype(jnp.float32)
    output = (middle + mlp_mix).astype(jnp.bfloat16)
    norm_one, router_one, kv_full, query_full, out_full, norm_two, router_two = fetch_layer()
    cot_float = cotangent.astype(jnp.float32)
    gate_grads = []
    up_grads = []
    down_grads = []
    wide_float = wide_cot.astype(jnp.float32)
    gate_terms = []
    for expert in range(mlp_experts):
        gate_pre, up_pre, inner_act, expert_out = saved_mlp[expert]
        gate_terms.append(jnp.sum(wide_float * expert_out, -1))
        d_expert = (wide_gate[:, expert : expert + 1] * wide_float).astype(jnp.bfloat16)
        d_inner = jnp.einsum(
            "td,fd->tf", d_expert, down_weight[expert], preferred_element_type=jnp.float32
        )
        d_gate_pre, d_up_pre = swiglu_back(d_inner, gate_pre, up_pre)
        step_grad = jnp.einsum(
            "tf,df->td", d_gate_pre, gate_weight[expert], preferred_element_type=jnp.float32
        ) + jnp.einsum("tf,df->td", d_up_pre, up_weight[expert], preferred_element_type=jnp.float32)
        wide_grad = step_grad if expert == 0 else wide_grad + step_grad
        gate_grads.append(
            jnp.einsum("td,tf->df", wide_normed, d_gate_pre, preferred_element_type=jnp.float32)
        )
        up_grads.append(
            jnp.einsum("td,tf->df", wide_normed, d_up_pre, preferred_element_type=jnp.float32)
        )
        down_grads.append(
            jnp.einsum("tf,td->fd", inner_act, d_expert, preferred_element_type=jnp.float32)
        )
    d_normed_two, d_gate_two = (
        lax.psum_scatter(wide_grad, "shard", scatter_dimension=0, tiled=True),
        lax.psum_scatter(jnp.stack(gate_terms, -1), "shard", scatter_dimension=0, tiled=True),
    )
    router_part_two, d_router_two = router_back(d_gate_two, gate_two, normed_two, router_two)
    d_normed_two = d_normed_two + router_part_two
    d_middle, d_norm_two = norm_back(d_normed_two, middle, scale_two, norm_two.astype(jnp.float32))
    d_middle = d_middle + cot_float
    d_gate_one = jnp.stack(
        [jnp.sum(d_middle * branch_list[expert], -1) for expert in range(att_experts)], -1
    )
    query_list = []
    branch_grads = []
    for expert in range(att_experts):
        d_branch = (gate_one[:, expert : expert + 1] * d_middle).astype(jnp.bfloat16)
        branch_grads.append(d_branch)
        d_heads = (
            jnp.einsum("td,fd->tf", d_branch, out_full[expert], preferred_element_type=jnp.float32)
            .astype(jnp.bfloat16)
            .reshape(row_count, head_count, HEAD)
        )
        row_top, row_total = row_stats[expert]
        scores = masked_scores(queries[expert])
        prob_float = jnp.exp(scores - row_top) / row_total
        prob_low = prob_float.astype(jnp.bfloat16)
        value_step = jnp.einsum(
            "hqk,qhd->khd", prob_low, d_heads, preferred_element_type=jnp.float32
        )
        d_prob = jnp.einsum("qhd,khd->hqk", d_heads, all_values, preferred_element_type=jnp.float32)
        d_scores = (prob_float * (d_prob - jnp.sum(prob_float * d_prob, -1, keepdims=True))).astype(
            jnp.bfloat16
        )
        query_step = (
            jnp.einsum("hqk,khd->qhd", d_scores, all_keys, preferred_element_type=jnp.float32)
            * score_scale
        )
        key_step = (
            jnp.einsum(
                "hqk,qhd->khd", d_scores, queries[expert], preferred_element_type=jnp.float32
            )
            * score_scale
        )
        key_total = key_step if expert == 0 else key_total + key_step
        value_total = value_step if expert == 0 else value_total + value_step
        d_query = (
            rotate(query_step, cos_table, sin_table, -1.0)
            .reshape(row_count, kv_width)
            .astype(jnp.bfloat16)
        )
        query_list.append(d_query)
        query_part = jnp.einsum(
            "tf,df->td", d_query, query_full[expert], preferred_element_type=jnp.float32
        )
        d_normed = query_part if expert == 0 else d_normed + query_part
    own_key_grad = key_total[reach_back * row_count :]
    own_value_grad = value_total[reach_back * row_count :]
    for offset in range(1, reach_back + 1):
        low_row = (reach_back - offset) * row_count
        back_key, back_value = (
            from_behind(
                key_total[low_row : low_row + row_count].astype(jnp.bfloat16), "shard", -offset
            ).astype(jnp.float32),
            from_behind(
                value_total[low_row : low_row + row_count].astype(jnp.bfloat16), "shard", -offset
            ).astype(jnp.float32),
        )
        own_key_grad = own_key_grad + back_key
        own_value_grad = own_value_grad + back_value
    d_keys = rotate(own_key_grad, cos_table, sin_table, -1.0)
    d_keyval = jnp.concatenate(
        [d_keys.reshape(row_count, kv_width), own_value_grad.reshape(row_count, kv_width)], -1
    ).astype(jnp.bfloat16)
    d_normed = d_normed + jnp.einsum(
        "tf,df->td", d_keyval, kv_full, preferred_element_type=jnp.float32
    )
    router_part_one, d_router_one = router_back(d_gate_one, gate_one, normed, router_one)
    d_normed = d_normed + router_part_one
    d_hidden, d_norm_one = norm_back(d_normed, hidden, scale_one, norm_one.astype(jnp.float32))
    input_grad = d_hidden + d_middle
    wide_rows, wide_keyval, wide_query, wide_heads, wide_branch = (
        lax.all_gather(normed, "shard", axis=0, tiled=True),
        lax.all_gather(d_keyval, "shard", axis=0, tiled=True),
        lax.all_gather(jnp.stack(query_list), "shard", axis=1, tiled=True),
        lax.all_gather(jnp.stack(heads_list), "shard", axis=1, tiled=True),
        lax.all_gather(jnp.stack(branch_grads), "shard", axis=1, tiled=True),
    )
    d_width = normed.shape[1] // shard_count
    h_width = kv_width // shard_count
    rows_own = lax.dynamic_slice_in_dim(wide_rows, shard_at * d_width, d_width, 1)
    heads_own = lax.dynamic_slice_in_dim(wide_heads, shard_at * h_width, h_width, 2)
    share_kv = jnp.einsum("td,tf->df", rows_own, wide_keyval, preferred_element_type=jnp.float32)
    share_query = jnp.einsum(
        "td,etf->edf", rows_own, wide_query, preferred_element_type=jnp.float32
    )
    share_out = jnp.einsum(
        "etf,etd->efd", heads_own, wide_branch, preferred_element_type=jnp.float32
    )
    share_norm_one, share_router_one, share_norm_two, share_router_two = (
        lax.psum_scatter(
            d_norm_one.astype(jnp.bfloat16), "shard", scatter_dimension=0, tiled=True
        ).astype(jnp.float32),
        lax.psum_scatter(
            d_router_one.astype(jnp.bfloat16), "shard", scatter_dimension=0, tiled=True
        ).astype(jnp.float32),
        lax.psum_scatter(
            d_norm_two.astype(jnp.bfloat16), "shard", scatter_dimension=0, tiled=True
        ).astype(jnp.float32),
        lax.psum_scatter(
            d_router_two.astype(jnp.bfloat16), "shard", scatter_dimension=0, tiled=True
        ).astype(jnp.float32),
    )
    expert_totals = (
        lax.psum_scatter(
            jnp.stack(gate_grads).astype(jnp.bfloat16), "rep", scatter_dimension=2, tiled=True
        ).astype(jnp.float32),
        lax.psum_scatter(
            jnp.stack(up_grads).astype(jnp.bfloat16), "rep", scatter_dimension=2, tiled=True
        ).astype(jnp.float32),
        lax.psum_scatter(
            jnp.stack(down_grads).astype(jnp.bfloat16), "rep", scatter_dimension=1, tiled=True
        ).astype(jnp.float32),
    )
    summed = (
        lax.psum(share_norm_one.astype(jnp.bfloat16), "rep").astype(jnp.float32),
        lax.psum(share_router_one.astype(jnp.bfloat16), "rep").astype(jnp.float32),
        lax.psum(share_kv.astype(jnp.bfloat16), "rep").astype(jnp.float32),
        lax.psum(share_query.astype(jnp.bfloat16), "rep").astype(jnp.float32),
        lax.psum(share_out.astype(jnp.bfloat16), "rep").astype(jnp.float32),
        lax.psum(share_norm_two.astype(jnp.bfloat16), "rep").astype(jnp.float32),
        lax.psum(share_router_two.astype(jnp.bfloat16), "rep").astype(jnp.float32),
    )
    return (
        output,
        input_grad,
        summed[0],
        summed[1],
        summed[2],
        summed[3],
        summed[4],
        summed[5],
        summed[6],
        expert_totals[0],
        expert_totals[1],
        expert_totals[2],
    )


def solution(mesh):
    return jax.shard_map(
        on_device,
        mesh=mesh,
        in_specs=(
            P(("rep", "shard"), None),
            P(("rep", "shard")),
            P("shard"),
            P("shard", None),
            P("shard", None),
            P(None, "shard", None),
            P(None, "shard", None),
            P("shard"),
            P("shard", None),
            P(None, None, "shard"),
            P(None, None, "shard"),
            P(None, "shard", None),
            P(("rep", "shard"), None),
        ),
        out_specs=(
            P(("rep", "shard"), None),
            P(("rep", "shard"), None),
            P("shard"),
            P("shard", None),
            P("shard", None),
            P(None, "shard", None),
            P(None, "shard", None),
            P("shard"),
            P("shard", None),
            P(None, None, ("shard", "rep")),
            P(None, None, ("shard", "rep")),
            P(None, ("shard", "rep"), None),
        ),
        check_vma=False,
    )
```

profile of v0, /device:TPU:0, one launch (start us, length us, event | category | flops | bytes accessed | tf_op | source)
XLA Modules:
  0.0 2933.6 jit_solution(9455951344299077646)
XLA Ops:
  51.5 118.6 %all-gather.14.cloned.1.call-done = bf16[2048,4096]{1,0:T(8,128)(2,1)} async-done(((bf16[512,4096]{1,0:T(8,128)(2,1)}), bf16[2048,4096]{1,0:T(8,128)(2,1)}) %all-gather.14.cloned.1.call-update) | async-done | bytes 16777232 | tf_op jit(solution)/shard_map/all_gather | solution.py:92
  210.3 243.9 %all-gather.16.cloned.1.call-done = bf16[2,2048,2048]{2,1,0:T(8,128)(2,1)} async-done(((bf16[2,512,2048]{2,1,0:T(8,128)(2,1)}), bf16[2,2048,2048]{2,1,0:T(8,128)(2,1)}) %all-gather.16.cloned.1.call-update) | async-done | bytes 16777232 | tf_op jit(solution)/shard_map/all_gather | solution.py:93
  490.0 20.6 fusion.149
  510.6 20.0 fusion.148
  530.6 17.8 collective-permute-done
  548.4 18.0 fusion.99
  566.4 82.3 %all-gather.18.cloned.1.call-done = bf16[2,2048,2048]{2,1,0:T(8,128)(2,1)} async-done(((bf16[2,512,2048]{2,1,0:T(8,128)(2,1)}), bf16[2,2048,2048]{2,1,0:T(8,128)(2,1)}) %all-gather.18.cloned.1.call-update) | async-done | bytes 16777232 | tf_op jit(solution)/shard_map/all_gather | solution.py:94
  693.6 61.6 %all-gather.20.cloned.1.call-done = bf16[1536,2048]{1,0:T(8,128)(2,1)} async-done(((bf16[384,2048]{1,0:T(8,128)(2,1)}), bf16[1536,2048]{1,0:T(8,128)(2,1)}) %all-gather.20.cloned.1.call-update) | async-done | bytes 6291472 | tf_op jit(solution)/shard_map/all_gather | solution.py:176
  786.1 41.0 %all-gather.22.cloned.1.call-done = bf16[1536,2048]{1,0:T(8,128)(2,1)} async-done(((bf16[384,2048]{1,0:T(8,128)(2,1)}), bf16[1536,2048]{1,0:T(8,128)(2,1)}) %all-gather.22.cloned.1.call-update) | async-done | bytes 6291472 | tf_op jit(solution)/shard_map/all_gather | solution.py:177
  827.1 23.3 multiply_convert_fusion.2
  895.4 23.7 multiply_convert_fusion.4
  962.5 20.9 fusion.12
  984.7 25.2 add_add_fusion
  1014.5 120.2 %reduce-scatter.15.cloned.1.call-done = f32[384,2048]{1,0:T(8,128)} async-done(((f32[1536,2048]{1,0:T(8,128)}), f32[384,2048]{1,0:T(8,128)}) %reduce-scatter.15.cloned.1.call-update) | async-done | bytes 3145744 | tf_op jit(solution)/shard_map/reduce_scatter | solution.py:223
  1141.1 67.3 %reduce-scatter.13.cloned.1.call-done = bf16[384,2048]{1,0:T(8,128)(2,1)} async-done(((bf16[1536,2048]{1,0:T(8,128)(2,1)}), bf16[384,2048]{1,0:T(8,128)(2,1)}) %reduce-scatter.13.cloned.1.call-update) | async-done | bytes 1572880 | tf_op jit(solution)/shard_map/reduce_scatter | solution.py:190
  1237.1 27.9 multiply_reduce_fusion
  1264.9 31.1 %multiply_convert_fusion = bf16[16,384,1536]{2,1,0:T(8,128)(2,1)} fusion(f32[16,384,1536]{2,1,0:T(8,128)} %get-tuple-element.131, f32[16,384]{1,0:T(8,128)S(1)} %get-tuple-element.130, f32[16,384,1536]{2,1,0:T(8,128)} %get-tuple-element.121, f32[16,384]{1,0:T(8,128)S(1)} %copy-done.60), kind=kLoop, calls=%fused_computation.2 | loop fusion | flops 37748736 | bytes 94420992 | tf_op jit(solution)/shard_map/convert_element_type | solution.py:251
  1296.1 26.6 multiply_reduce_fusion.1
  1334.1 31.1 %multiply_convert_fusion.1 = bf16[16,384,1536]{2,1,0:T(8,128)(2,1)} fusion(f32[16,384,1536]{2,1,0:T(8,128)} %get-tuple-element.133, f32[16,384]{1,0:T(8,128)S(1)} %get-tuple-element.132, f32[16,384,1536]{2,1,0:T(8,128)} %get-tuple-element.123, f32[16,384]{1,0:T(8,128)S(1)} %copy-done.57), kind=kLoop, calls=%fused_computation.4 | loop fusion | flops 37748736 | bytes 94420992 | tf_op jit(solution)/shard_map/convert_element_type | solution.py:251
  1407.6 20.6 fusion.157
  1436.1 19.2 fusion.14
  1455.3 24.4 fusion.156
  1488.8 44.1 %collective-permute-done.7 = bf16[384,16,128]{2,0,1:T(8,128)(2,1)} collective-permute-done((bf16[384,16,128]{2,0,1:T(8,128)(2,1)S(1)}, bf16[384,16,128]{2,0,1:T(8,128)(2,1)}, u32[]{:S(2)}, u32[]{:S(2)}) %collective-permute-start.7) | collective-permute-done | bytes 1572896 | tf_op jit(solution)/shard_map/ppermute | solution.py:18
  1540.1 59.9 %collective-permute-done.11 = bf16[384,16,128]{0,2,1:T(8,128)(2,1)} collective-permute-done((bf16[384,16,128]{0,2,1:T(8,128)(2,1)}, bf16[384,16,128]{0,2,1:T(8,128)(2,1)}, u32[]{:S(2)}, u32[]{:S(2)}) %collective-permute-start.11) | collective-permute-done | bytes 1572896 | tf_op jit(solution)/shard_map/ppermute | solution.py:18
  1600.0 33.0 %collective-permute-done.10 = bf16[384,16,128]{0,2,1:T(8,128)(2,1)} collective-permute-done((bf16[384,16,128]{0,2,1:T(8,128)(2,1)}, bf16[384,16,128]{0,2,1:T(8,128)(2,1)}, u32[]{:S(2)}, u32[]{:S(2)}) %collective-permute-start.10) | collective-permute-done | bytes 1572896 | tf_op jit(solution)/shard_map/ppermute | solution.py:18
  1761.9 29.5 %copy.107 = bf16[2,2048,1408]{1,0,2:T(2,128)(2,1)} copy(bf16[2,2048,1408]{2,1,0:T(8,128)(2,1)} %pad_maximum_fusion) | data formatting | bytes 23068672 | tf_op jit(solution)/shard_map/stack | solution.py:335
  1822.6 29.3 copy.108
  1877.2 19.1 all-gather.30.cloned.1.call-done
  1896.3 124.4 %all-gather.32.cloned.1.call-done = bf16[2,1536,2048]{2,1,0:T(8,128)(2,1)} async-done(((bf16[2,384,2048]{2,1,0:T(8,128)(2,1)}), bf16[2,1536,2048]{2,1,0:T(8,128)(2,1)}) %all-gather.32.cloned.1.call-update) | async-done | bytes 12582928 | tf_op jit(solution)/shard_map/all_gather | solution.py:306
  2049.7 120.6 %reduce-scatter.17.cloned.1.call-done = bf16[2,176,2048]{2,1,0:T(8,128)(2,1)} async-done(((bf16[2,1408,2048]{2,1,0:T(8,128)(2,1)}), bf16[2,176,2048]{2,1,0:T(8,128)(2,1)}) %reduce-scatter.17.cloned.1.call-update) | async-done | bytes 1441808 | tf_op jit(solution)/shard_map/reduce_scatter | solution.py:340
  2173.6 23.4 reduce-scatter.21.cloned.1.call-done
  2224.9 669.1 %all-reduce.9.cloned.1.call-done = (bf16[2,512,2048]{1,2,0:T(8,128)(2,1)}, bf16[512,4096]{1,0:T(8,128)(2,1)}, bf16[2,512,2048]{2,1,0:T(8,128)(2,1)}, bf16[2,2048,1408]{1,0,2:T(2,128)(2,1)}, bf16[2,2048,1408]{1,0,2:T(2,128)(2,1)}) async-done(((bf16[2,512,2048]{1,2,0:T(8,128)(2,1)}, bf16[512,4096]{1,0:T(8,128)(2,1)}, bf16[2,512,2048]{2,1,0:T(8,128)(2,1)}, bf16[2,2048,1408]{1,0,2:T(2,128)(2,1)}, ...) | async-done | bytes 35651600 | tf_op jit(solution)/shard_map/psum | solution.py:348
  (433 shorter events, 678.5 us)
Async XLA Ops:
  7.2 162.9 %all-gather.14.cloned.1.call-start = ((), (), s32[]{:S(2)}) async-start(), calls=%async_computation.6 | async-start | bytes 20971520 | tf_op jit(solution)/shard_map/all_gather | solution.py:92
  8.0 446.3 %all-gather.16.cloned.1.call-start = ((), (), s32[]{:S(2)}) async-start(), calls=%async_computation.7 | async-start | bytes 20971520 | tf_op jit(solution)/shard_map/all_gather | solution.py:93
  8.7 640.0 %all-gather.18.cloned.1.call-start = ((), (), s32[]{:S(2)}) async-start(), calls=%async_computation.8 | async-start | bytes 20971520 | tf_op jit(solution)/shard_map/all_gather | solution.py:94
  9.5 745.8 %all-gather.20.cloned.1.call-start = ((), (), s32[]{:S(2)}) async-start(), calls=%async_computation.9 | async-start | bytes 7864320 | tf_op jit(solution)/shard_map/all_gather | solution.py:176
  46.2 408.0 %copy-start.7 = (bf16[384,2048]{1,0:T(8,128)(2,1)}, bf16[384,2048]{1,0:T(8,128)(2,1)S(1)}, u32[]{:S(2)}) copy-start(bf16[384,2048]{1,0:T(8,128)(2,1)S(1)} %fusion.77) | copy-start | bytes 4718596
  49.0 425.0 %copy-start.22 = (f32[384,64]{1,0:T(8,128)}, f32[384,64]{1,0:T(8,128)S(1)}, u32[]{:S(2)}) copy-start(f32[384,64]{1,0:T(8,128)S(1)} %get-tuple-element.112) | copy-start | bytes 294916
  49.0 425.0 %copy-start.25 = (f32[384,64]{1,0:T(8,128)}, f32[384,64]{1,0:T(8,128)S(1)}, u32[]{:S(2)}) copy-start(f32[384,64]{1,0:T(8,128)S(1)} %get-tuple-element.113) | copy-start | bytes 294916
  185.6 345.0 %collective-permute-start.2 = (bf16[384,16,128]{0,2,1:T(8,128)(2,1)}, bf16[384,16,128]{0,2,1:T(8,128)(2,1)}, u32[]{:S(2)}, u32[]{:S(2)}) collective-permute-start(bf16[384,16,128]{0,2,1:T(8,128)(2,1)} %bitcast.45), channel_id=1, source_target_pairs={{0,1},{1,2},{2,3},{4,5},{5,6},{6,7},{8,9},{9,10},{10,11},{12,13},{... | collective-permute-start | bytes 4718600 | tf_op jit(solution)/shard_map/ppermute | solution.py:18
  190.2 340.4 %collective-permute-start.1 = (bf16[384,16,128]{0,2,1:T(8,128)(2,1)}, bf16[384,16,128]{0,2,1:T(8,128)(2,1)}, u32[]{:S(2)}, u32[]{:S(2)}) collective-permute-start(bf16[384,16,128]{0,2,1:T(8,128)(2,1)} %bitcast.45), channel_id=1, source_target_pairs={{0,2},{1,3},{4,6},{5,7},{8,10},{9,11},{12,14},{13,15},{16,18},{17,... | collective-permute-start | bytes 4718600 | tf_op jit(solution)/shard_map/ppermute | solution.py:18
  202.0 285.1 %collective-permute-start.5 = (bf16[384,16,128]{2,0,1:T(8,128)(2,1)}, bf16[384,16,128]{2,0,1:T(8,128)(2,1)}, u32[]{:S(2)}, u32[]{:S(2)}) collective-permute-start(bf16[384,16,128]{2,0,1:T(8,128)(2,1)} %pad_maximum_fusion.9), channel_id=1, source_target_pairs={{0,1},{1,2},{2,3},{4,5},{5,6},{6,7},{8,9},{9,10},{10,11},{12,13},{... | collective-permute-start | bytes 4718600 | tf_op jit(solution)/shard_map/ppermute | solution.py:18
  205.3 284.7 %collective-permute-start.4 = (bf16[384,16,128]{2,0,1:T(8,128)(2,1)}, bf16[384,16,128]{2,0,1:T(8,128)(2,1)}, u32[]{:S(2)}, u32[]{:S(2)}) collective-permute-start(bf16[384,16,128]{2,0,1:T(8,128)(2,1)} %pad_maximum_fusion.9), channel_id=1, source_target_pairs={{0,2},{1,3},{4,6},{5,7},{8,10},{9,11},{12,14},{13,15},{16,18},{17,... | collective-permute-start | bytes 4718600 | tf_op jit(solution)/shard_map/ppermute | solution.py:18
  207.7 282.3 %collective-permute-start.3 = (bf16[384,16,128]{2,0,1:T(8,128)(2,1)}, bf16[384,16,128]{2,0,1:T(8,128)(2,1)}, u32[]{:S(2)}, u32[]{:S(2)}) collective-permute-start(bf16[384,16,128]{2,0,1:T(8,128)(2,1)} %pad_maximum_fusion.9), channel_id=1, source_target_pairs={{0,3},{4,7},{8,11},{12,15},{16,19},{20,23},{24,27},{28,31}} | collective-permute-start | bytes 4718600 | tf_op jit(solution)/shard_map/ppermute | solution.py:18
  487.1 61.3 %collective-permute-start = (bf16[384,16,128]{0,2,1:T(8,128)(2,1)}, bf16[384,16,128]{0,2,1:T(8,128)(2,1)}, u32[]{:S(2)}, u32[]{:S(2)}) collective-permute-start(bf16[384,16,128]{0,2,1:T(8,128)(2,1)} %bitcast.45), channel_id=1, source_target_pairs={{0,3},{4,7},{8,11},{12,15},{16,19},{20,23},{24,27},{28,31}} | collective-permute-start | bytes 4718600 | tf_op jit(solution)/shard_map/ppermute | solution.py:18
  684.9 142.2 %all-gather.22.cloned.1.call-start = ((), (), s32[]{:S(2)}) async-start(), calls=%async_computation.11 | async-start | bytes 7864320 | tf_op jit(solution)/shard_map/all_gather | solution.py:177
  685.5 327.9 %reduce-scatter.19.cloned.1.call-start = ((), (), s32[]{:S(2)}) async-start(), calls=%async_computation.19 | async-start | bytes 983040
  984.6 150.1 %reduce-scatter.15.cloned.1.call-start = ((), (), s32[]{:S(2)}) async-start(), calls=%async_computation.12 | async-start | bytes 15728640 | tf_op jit(solution)/shard_map/reduce_scatter | solution.py:223
  1009.9 198.6 %reduce-scatter.13.cloned.1.call-start = ((), (), s32[]{:S(2)}) async-start(), calls=%async_computation.10 | async-start | bytes 7864320 | tf_op jit(solution)/shard_map/reduce_scatter | solution.py:190
  1010.6 843.2 %all-gather.24.cloned.1.call-start = ((), (), s32[]{:S(2)}) async-start(), calls=%async_computation.13 | async-start | bytes 7864320 | tf_op jit(solution)/shard_map/all_gather | solution.py:302
  1011.4 842.5 %all-gather.28.cloned.1.call-start = ((), (), s32[]{:S(2)}) async-start(), calls=%async_computation.15 | async-start | bytes 15728640 | tf_op jit(solution)/shard_map/all_gather | solution.py:304
  1393.6 472.1 %all-gather.26.cloned.1.call-start = ((), (), s32[]{:S(2)}) async-start(), calls=%async_computation.14 | async-start | bytes 15728640 | tf_op jit(solution)/shard_map/all_gather | solution.py:303
  1432.2 55.0 %collective-permute-start.8 = (bf16[384,16,128]{2,0,1:T(8,128)(2,1)}, bf16[384,16,128]{2,0,1:T(8,128)(2,1)}, u32[]{:S(2)}, u32[]{:S(2)}) collective-permute-start(bf16[384,16,128]{2,0,1:T(8,128)(2,1)} %get-tuple-element.89), channel_id=1, source_target_pairs={{3,0},{7,4},{11,8},{15,12},{19,16},{23,20},{27,24},{31,28}} | collective-permute-start | bytes 4718600 | tf_op jit(solution)/shard_map/ppermute | solution.py:18
  1433.4 99.5 %collective-permute-start.7 = (bf16[384,16,128]{2,0,1:T(8,128)(2,1)S(1)}, bf16[384,16,128]{2,0,1:T(8,128)(2,1)}, u32[]{:S(2)}, u32[]{:S(2)}) collective-permute-start(bf16[384,16,128]{2,0,1:T(8,128)(2,1)S(1)} %get-tuple-element.90), channel_id=1, source_target_pairs={{2,0},{3,1},{6,4},{7,5},{10,8},{11,9},{14,12},{15,13},{18,16},{19,... | collective-permute-start | bytes 4718600 | tf_op jit(solution)/shard_map/ppermute | solution.py:18
  1434.8 98.2 %collective-permute-start.6 = (bf16[384,16,128]{2,0,1:T(8,128)(2,1)S(1)}, bf16[384,16,128]{2,0,1:T(8,128)(2,1)}, u32[]{:S(2)}, u32[]{:S(2)}) collective-permute-start(bf16[384,16,128]{2,0,1:T(8,128)(2,1)S(1)} %get-tuple-element.88), channel_id=1, source_target_pairs={{1,0},{2,1},{3,2},{5,4},{6,5},{7,6},{9,8},{10,9},{11,10},{13,12},{... | collective-permute-start | bytes 4718600 | tf_op jit(solution)/shard_map/ppermute | solution.py:18
  1484.5 115.5 %collective-permute-start.11 = (bf16[384,16,128]{0,2,1:T(8,128)(2,1)}, bf16[384,16,128]{0,2,1:T(8,128)(2,1)}, u32[]{:S(2)}, u32[]{:S(2)}) collective-permute-start(bf16[384,16,128]{0,2,1:T(8,128)(2,1)} %get-tuple-element.92), channel_id=1, source_target_pairs={{3,0},{7,4},{11,8},{15,12},{19,16},{23,20},{27,24},{31,28}} | collective-permute-start | bytes 4718600 | tf_op jit(solution)/shard_map/ppermute | solution.py:18
  1485.8 147.3 %collective-permute-start.10 = (bf16[384,16,128]{0,2,1:T(8,128)(2,1)}, bf16[384,16,128]{0,2,1:T(8,128)(2,1)}, u32[]{:S(2)}, u32[]{:S(2)}) collective-permute-start(bf16[384,16,128]{0,2,1:T(8,128)(2,1)} %get-tuple-element.93), channel_id=1, source_target_pairs={{2,0},{3,1},{6,4},{7,5},{10,8},{11,9},{14,12},{15,13},{18,16},{19,... | collective-permute-start | bytes 4718600 | tf_op jit(solution)/shard_map/ppermute | solution.py:18
  1487.1 146.0 %collective-permute-start.9 = (bf16[384,16,128]{0,2,1:T(8,128)(2,1)}, bf16[384,16,128]{0,2,1:T(8,128)(2,1)}, u32[]{:S(2)}, u32[]{:S(2)}) collective-permute-start(bf16[384,16,128]{0,2,1:T(8,128)(2,1)} %get-tuple-element.91), channel_id=1, source_target_pairs={{1,0},{2,1},{3,2},{5,4},{6,5},{7,6},{9,8},{10,9},{11,10},{13,12},{... | collective-permute-start | bytes 4718600 | tf_op jit(solution)/shard_map/ppermute | solution.py:18
  1640.5 255.8 %all-gather.30.cloned.1.call-start = ((), (), s32[]{:S(2)}) async-start(), calls=%async_computation.16 | async-start | bytes 15728640 | tf_op jit(solution)/shard_map/all_gather | solution.py:305
  1644.6 376.0 %all-gather.32.cloned.1.call-start = ((), (), s32[]{:S(2)}) async-start(), calls=%async_computation.17 | async-start | bytes 15728640 | tf_op jit(solution)/shard_map/all_gather | solution.py:306
  1688.7 360.0 %reduce-scatter.23.cloned.1.call-start = ((), (), s32[]{:S(2)}) async-start(), calls=%async_computation.21 | async-start | bytes 655360
  1720.4 449.9 %reduce-scatter.17.cloned.1.call-start = ((), (), s32[]{:S(2)}) async-start(), calls=%async_computation.18 | async-start | bytes 12976128 | tf_op jit(solution)/shard_map/reduce_scatter | solution.py:340
  1730.5 466.5 %reduce-scatter.21.cloned.1.call-start = ((), (), s32[]{:S(2)}) async-start(), calls=%async_computation.20 | async-start | bytes 655360
  1853.8 1040.2 %all-reduce.9.cloned.1.call-start = ((), (), s32[]{:S(2)}) async-start(), calls=%async_computation.22 | async-start | bytes 71303168 | tf_op jit(solution)/shard_map/psum | solution.py:348
  (111 other events, 3503.9 us)
Sparse Core Ops, SparseCore 0:
  9.8 160.2 all-gather.13
  172.0 282.2 all-gather.15
  456.1 192.5 all-gather.17
  685.1 70.1 all-gather.19
  756.9 70.1 all-gather.21
  984.7 26.0 reduce-scatter.18
  1014.0 120.6 reduce-scatter.14
  1138.3 70.1 reduce-scatter.12
  1210.3 70.1 all-gather.23
  1393.7 249.0 all-gather.27
  1644.7 127.4 all-gather.25
  1773.8 122.3 all-gather.29
  1898.1 122.5 all-gather.31
  2023.9 24.7 reduce-scatter.22
  2051.0 119.2 reduce-scatter.16
  2173.8 23.1 reduce-scatter.20
  2200.6 693.3 all-reduce.8
where the time goes:
time: 2940 us; the launch traced here: 2930 us
  waiting for transfers between devices  1860 us (63%)
  matrix products  659 us (22%)
  other arithmetic  178 us (6%)
  local copies, waits for them, and re-layouts  125 us (4%)
  blocking collectives  65.1 us (2%)
    psum x1, waiting for transfers between devices, on_device(): lax.psum(share_query.astype(jnp.bfloat16), 'rep').astype(jnp.float32)  669 us
    all_gather x1, waiting for transfers between devices, fetch_layer(): lax.all_gather(query_weight, 'shard', axis=1, tiled=True)  244 us
    ppermute x12, waiting for transfers between devices, from_behind(): lax.ppermute(value, axis, [(source, source + steps) for source in range(i...  155 us
    all_gather x1, waiting for transfers between devices, on_device(): lax.all_gather(jnp.stack(branch_grads), 'shard', axis=1, tiled=True)  124 us
    reduce_scatter x1, waiting for transfers between devices, on_device(): lax.psum_scatter(jnp.stack(down_grads).astype(jnp.bfloat16), 'rep', scatt...  121 us
    reduce_scatter x1, waiting for transfers between devices, on_device(): lax.psum_scatter(wide_grad, 'shard', scatter_dimension=0, tiled=True)  120 us
    all_gather x1, waiting for transfers between devices, fetch_layer(): lax.all_gather(kv_weight, 'shard', axis=0, tiled=True)  119 us
    all_gather x1, waiting for transfers between devices, fetch_layer(): lax.all_gather(out_weight, 'shard', axis=1, tiled=True)  82.3 us
  transfers between devices with their start and end apart: 29, of which 17 were waited for; matrix products, arithmetic and copies ran while one was open for 25% of the time, Pallas kernels for 0%

commit v1 on v0

v1 whole, which is shorter than its diff:
```python
import jax
import jax.numpy as jnp
from jax import lax
from jax.experimental import pallas as pl
from jax.experimental.pallas import tpu as pltpu
from jax.sharding import Mesh, PartitionSpec as P

HEAD = 128
WIN = 1024
EPSILON = 1e-06
THETA = 10000.0
HIGHEST = lax.Precision.HIGHEST
BF16 = jnp.bfloat16
F32 = jnp.float32
LOG2E = 1.4426950408889634
MIB = 1 << 20
QUERY_ROWS = 256


def swap(value, axis, bits):
    count = lax.axis_size(axis)
    return lax.ppermute(value, axis, [(i, i ^ bits) for i in range(count)])


def together(*values):
    return lax.optimization_barrier(values)


def bit_orders(count):
    bits = [1 << b for b in range(count.bit_length() - 1)]
    return [bits[i:] + bits[:i] for i in range(len(bits))] or [[]]


def ways(held, axis):
    orders = bit_orders(lax.axis_size(axis))
    return [(orders[i % len(orders)], part) for i, part in enumerate(held)]


def gather_start(block, axis="shard"):
    orders = bit_orders(lax.axis_size(axis))
    return [{0: part} for part in together(*jnp.split(block, len(orders), 0))]


def gather_step(held, step, axis="shard"):
    after = []
    for order, have in ways(held, axis):
        bit = order[step]
        after.append({**have, **{r ^ bit: swap(v, axis, bit) for r, v in have.items()}})
    return after


def gather_end(held):
    return [jnp.concatenate([have[r] for have in held], 0) for r in range(len(held[0]))]


def gather_blocks(block, axis="shard"):
    held = gather_start(block, axis)
    for step in range(len(bit_orders(lax.axis_size(axis))[0])):
        held = gather_step(held, step, axis)
    return gather_end(held)


def scatter_start(blocks, axis="shard"):
    orders = bit_orders(lax.axis_size(axis))
    held = [dict() for _ in orders]
    for r, block in enumerate(blocks):
        for have, part in zip(held, jnp.split(block, len(orders), 0)):
            have[r] = part
    return held


def scatter_cut(held, step, axis="shard"):
    cut = []
    for order, have in ways(held, axis):
        bit = order[-1 - step]
        kept = {r: v for r, v in have.items() if not r & bit}
        cut.append((kept, jnp.concatenate([have[r ^ bit].astype(BF16) for r in kept], 0)))
    sent = together(*[sent for _, sent in cut])
    return [(kept, new) for (kept, _), new in zip(cut, sent)]


def scatter_send(cut, step, axis="shard"):
    pairs = []
    for order, (kept, sent) in ways(cut, axis):
        pairs.append((kept, swap(sent, axis, order[-1 - step])))
    return pairs


def arrived(pairs, *beside):
    got, *beside = together([got for _, got in pairs], *beside)
    return [(kept, new) for (kept, _), new in zip(pairs, got)], *beside


def scatter_step(held, step, axis="shard"):
    return scatter_send(scatter_cut(held, step, axis), step, axis)


def scatter_add(pairs):
    held = []
    for kept, got in pairs:
        got = jnp.split(got, len(kept), 0)
        held.append({r: kept[r].astype(F32) + new.astype(F32) for r, new in zip(kept, got)})
    return held


def scatter_end(held):
    return jnp.concatenate([have[0] for have in held], 0)


def scatter_sum(blocks, beside=(), axis="shard"):
    held = scatter_start(blocks, axis)
    beside = list(beside)
    for step in range(len(bit_orders(lax.axis_size(axis))[0])):
        pairs = scatter_step(held, step, axis)
        if step < len(beside):
            pairs, beside[step] = arrived(pairs, beside[step])
        held = scatter_add(pairs)
    return scatter_end(held), beside


def scatter_small(blocks, axis="shard"):
    total = blocks[0]
    for r in range(1, lax.axis_size(axis)):
        total = total + swap(blocks[r], axis, r)
    return total


REPLICAS = ("chip", "core")


def replica_scatter(whole):
    return lax.psum_scatter(whole, REPLICAS, scatter_dimension=1, tiled=True)


def chip_sum(whole, axis):
    core = lax.axis_index("core")
    kept = lax.dynamic_index_in_dim(whole, core, axis, keepdims=False)
    sent = lax.dynamic_index_in_dim(whole, 1 - core, axis, keepdims=False)
    return kept, swap(sent, "core", 1)


def add_low(kept, got):
    return (kept.astype(F32) + got.astype(F32)).astype(BF16)


def pick(options, index):
    chosen = options[0]
    for i, option in enumerate(options[1:], 1):
        chosen = jnp.where(index == i, option, chosen)
    return chosen


def in_order(blocks, me, base=None):
    rows = blocks[0].shape[0]
    whole = base
    if base is None:
        whole = jnp.zeros((rows * len(blocks),) + blocks[0].shape[1:], blocks[0].dtype)
    for r, block in enumerate(blocks):
        start = ((me ^ r) * rows,) + (0,) * (block.ndim - 1)
        whole = lax.dynamic_update_slice(whole, block, start)
    return whole


def by_distance(whole, me, count):
    rows = whole.shape[0] // count
    return [lax.dynamic_slice_in_dim(whole, (me ^ r) * rows, rows, 0) for r in range(count)]


def rotation_tables(length):
    half = HEAD // 2
    frequency = THETA ** (-jnp.arange(half, dtype=F32) / half)
    angle = jnp.arange(length, dtype=F32)[:, None] * frequency[None, :]
    cos, sin = jnp.cos(angle), jnp.sin(angle)
    return jnp.concatenate([cos, cos], 1), jnp.concatenate([-sin, sin], 1)


def turn(head, cos, sin):
    return head * cos + pltpu.roll(head, HEAD // 2, 1) * sin


def nt(a, b):
    return lax.dot_general(a, b, (((1,), (1,)), ((), ())), preferred_element_type=F32)


def nn(a, b):
    return lax.dot_general(a, b, (((1,), (0,)), ((), ())), preferred_element_type=F32)


def tn(a, b):
    return lax.dot_general(a, b, (((0,), (0,)), ((), ())), preferred_element_type=F32)


def project_kernel(normed, weight, cos, sin, out):
    kind = pl.program_id(1)
    product = nn(normed[...], weight[0])

    @pl.when(kind == 1)
    def _():
        out[0] = product.astype(BF16)

    @pl.when(kind != 1)
    def _():
        for start in range(0, product.shape[1], HEAD):
            head = product[:, start : start + HEAD]
            out[0, :, start : start + HEAD] = turn(head, cos[...], sin[...]).astype(BF16)


def project(normed, weight, cos, sin):
    seq, width = normed.shape
    kinds, _, cols = weight.shape
    rows = seq
    once = dict(pipeline_mode=pl.Buffered(1))
    return pl.pallas_call(
        project_kernel,
        grid=(seq // rows, kinds),
        in_specs=[
            pl.BlockSpec((rows, width), lambda i, k: (i, 0), **once),
            pl.BlockSpec((1, width, cols), lambda i, k: (k, 0, 0)),
            pl.BlockSpec((rows, HEAD), lambda i, k: (i, 0), **once),
            pl.BlockSpec((rows, HEAD), lambda i, k: (i, 0), **once),
        ],
        out_specs=pl.BlockSpec((1, rows, cols), lambda i, k: (k, i, 0)),
        out_shape=jax.ShapeDtypeStruct((kinds, seq, cols), BF16),
        compiler_params=pltpu.CompilerParams(vmem_limit_bytes=48 * MIB),
        cost_estimate=pl.CostEstimate(
            flops=2 * seq * width * kinds * cols,
            bytes_accessed=2 * (seq * width + kinds * cols * (width + seq)),
            transcendentals=0,
        ),
    )(normed, weight, cos, sin)


def key_span(block):
    low = max(0, block * QUERY_ROWS - WIN + 1) // QUERY_ROWS * QUERY_ROWS
    return low, (block + 1) * QUERY_ROWS


def forbid(query_segment, key_segment, query_place, key_place):
    distance = query_place - key_place
    allowed = (query_segment == key_segment) & (distance >= 0) & (distance < WIN)
    return jnp.where(allowed, 0.0, -1e30).astype(F32)


def attend_kernel(experts, blocks, seg_col, seg_row, keys, values, *rest):
    queries, (out, stats, bias) = rest[:experts], rest[experts:]
    block, head = pl.program_id(0), pl.program_id(1)
    factor = HEAD ** (-0.5) * LOG2E
    rows = experts * QUERY_ROWS

    def step(at):
        low, high = key_span(at)
        span = high - low

        @pl.when(head == 0)
        def _():
            shape = (QUERY_ROWS, span)
            bias[:, :span] = forbid(
                seg_col[...],
                seg_row[:, low:high],
                at * QUERY_ROWS + lax.broadcasted_iota(jnp.int32, shape, 0),
                low + lax.broadcasted_iota(jnp.int32, shape, 1),
            )

        query = jnp.concatenate([q[0] for q in queries], 0)
        scores = nt(query, keys[0, low:high])
        scores = scores + jnp.concatenate([bias[:, :span]] * experts, 0)
        top = jnp.max(scores, -1, keepdims=True)
        weights = jnp.exp2((scores - top) * factor)
        total = jnp.sum(weights, -1, keepdims=True)
        mixed = nn(weights.astype(BF16), values[0, low:high]) / total
        level = jnp.broadcast_to(top * factor + jnp.log2(total), (rows, HEAD)).T
        for expert in range(experts):
            part = slice(expert * QUERY_ROWS, (expert + 1) * QUERY_ROWS)
            out[expert] = mixed[part].astype(BF16)
            stats[0, expert : expert + 1, :] = level[0:1, part]

    for at in range(blocks):
        pl.when(block == at)(lambda at=at: step(at))


def attend(projected, segments):
    kinds, seq, cols = projected.shape
    experts, heads, blocks = kinds - 2, cols // HEAD, seq // QUERY_ROWS
    widest = max(high - low for low, high in map(key_span, range(blocks)))
    pairs = sum(high - low for low, high in map(key_span, range(blocks))) * QUERY_ROWS
    query_specs = [
        pl.BlockSpec((1, QUERY_ROWS, HEAD), lambda i, h, e=e: (2 + e, i, h)) for e in range(experts)
    ]
    return pl.pallas_call(
        lambda *refs: attend_kernel(experts, blocks, *refs),
        grid=(blocks, heads),
        in_specs=[
            pl.BlockSpec((QUERY_ROWS, 1), lambda i, h: (i, 0)),
            pl.BlockSpec((1, seq), lambda i, h: (0, 0)),
            pl.BlockSpec((1, seq, HEAD), lambda i, h: (0, 0, h)),
            pl.BlockSpec((1, seq, HEAD), lambda i, h: (1, 0, h)),
        ]
        + query_specs,
        out_specs=[
            pl.BlockSpec((experts, QUERY_ROWS, HEAD), lambda i, h: (0, i, h)),
            pl.BlockSpec((1, experts, QUERY_ROWS), lambda i, h: (h, 0, i)),
        ],
        out_shape=[
            jax.ShapeDtypeStruct((experts, seq, cols), BF16),
            jax.ShapeDtypeStruct((heads, experts, seq), F32),
        ],
        scratch_shapes=[pltpu.VMEM((QUERY_ROWS, widest), F32)],
        compiler_params=pltpu.CompilerParams(vmem_limit_bytes=48 * MIB),
        cost_estimate=pl.CostEstimate(
            flops=8 * pairs * experts * heads * HEAD,
            bytes_accessed=2 * seq * cols * (2 + 2 * experts),
            transcendentals=pairs * experts * heads,
        ),
    )(segments[:, None], segments[None, :], *([projected] * (2 + experts)))


def attend_back_kernel(experts, blocks, seg_row, seg_col, cos, sin, keys, values, *rest):
    queries = rest[:experts]
    d_heads, stats, delta, out, bias, d_keys, d_values = rest[experts:]
    head, block = pl.program_id(0), pl.program_id(1)
    scale = HEAD ** (-0.5)
    factor = scale * LOG2E

    @pl.when(block == 0)
    def _():
        d_keys[...] = jnp.zeros_like(d_keys)
        d_values[...] = jnp.zeros_like(d_values)

    def step(at):
        low, high = key_span(at)
        span = high - low
        own = slice(at * QUERY_ROWS, (at + 1) * QUERY_ROWS)

        @pl.when(head == 0)
        def _():
            shape = (span, QUERY_ROWS)
            bias[at, :span, :] = forbid(
                seg_row[...],
                seg_col[low:high],
                at * QUERY_ROWS + lax.broadcasted_iota(jnp.int32, shape, 1),
                low + lax.broadcasted_iota(jnp.int32, shape, 0),
            )

        for expert in range(experts):
            query = queries[expert][0]
            d_head = d_heads[expert]
            key, value = keys[0, low:high], values[0, low:high]
            scores = nt(key, query) * factor + bias[at, :span, :]
            probs = jnp.exp2(scores - stats[0, expert : expert + 1, :])
            d_probs = nt(value, d_head)
            d_scores = (probs * (d_probs - delta[0, expert : expert + 1, :])).astype(BF16)
            d_values[low:high] += nn(probs.astype(BF16), d_head)
            d_keys[low:high] += nn(d_scores, query)
            d_query = tn(d_scores, key) * scale
            out[2 + expert, own, :] = turn(d_query, cos[own], -sin[own]).astype(BF16)

    for at in range(blocks):
        pl.when(block == at)(lambda at=at: step(at))

    @pl.when(block == blocks - 1)
    def _():
        out[0] = turn(d_keys[...] * scale, cos[...], -sin[...]).astype(BF16)
        out[1] = d_values[...].astype(BF16)


def attend_back(projected, segments, cos, sin, d_heads, stats, delta):
    kinds, seq, cols = projected.shape
    experts, heads, blocks = kinds - 2, cols // HEAD, seq // QUERY_ROWS
    widest = max(high - low for low, high in map(key_span, range(blocks)))
    pairs = sum(high - low for low, high in map(key_span, range(blocks))) * QUERY_ROWS
    query_specs = [
        pl.BlockSpec((1, QUERY_ROWS, HEAD), lambda h, i, e=e: (2 + e, i, h)) for e in range(experts)
    ]
    row_spec = pl.BlockSpec((1, experts, QUERY_ROWS), lambda h, i: (h, 0, i))
    return pl.pallas_call(
        lambda *refs: attend_back_kernel(experts, blocks, *refs),
        grid=(heads, blocks),
        in_specs=[
            pl.BlockSpec((1, QUERY_ROWS), lambda h, i: (0, i)),
            pl.BlockSpec((seq, 1), lambda h, i: (0, 0)),
            pl.BlockSpec((seq, HEAD), lambda h, i: (0, 0)),
            pl.BlockSpec((seq, HEAD), lambda h, i: (0, 0)),
            pl.BlockSpec((1, seq, HEAD), lambda h, i: (0, 0, h)),
            pl.BlockSpec((1, seq, HEAD), lambda h, i: (1, 0, h)),
        ]
        + query_specs
        + [
            pl.BlockSpec((experts, QUERY_ROWS, HEAD), lambda h, i: (0, i, h)),
            row_spec,
            row_spec,
        ],
        out_specs=pl.BlockSpec((kinds, seq, HEAD), lambda h, i: (0, 0, h)),
        out_shape=jax.ShapeDtypeStruct((kinds, seq, cols), BF16),
        scratch_shapes=[
            pltpu.VMEM((blocks, widest, QUERY_ROWS), F32),
            pltpu.VMEM((seq, HEAD), F32),
            pltpu.VMEM((seq, HEAD), F32),
        ],
        compiler_params=pltpu.CompilerParams(vmem_limit_bytes=48 * MIB),
        cost_estimate=pl.CostEstimate(
            flops=20 * pairs * experts * heads * HEAD,
            bytes_accessed=2 * seq * cols * (2 * kinds + experts),
            transcendentals=pairs * experts * heads,
        ),
    )(
        segments[None, :],
        segments[:, None],
        cos,
        sin,
        *([projected] * (2 + experts)),
        d_heads,
        stats,
        delta,
    )


def norm_back(d_normed, hidden, inv_scale, gain):
    scaled_grad = d_normed * gain
    return inv_scale * scaled_grad - hidden * inv_scale**3 * jnp.mean(
        scaled_grad * hidden, -1, keepdims=True
    )


def swiglu_kernel(expert, gate_pre, up_pre, d_act, gates, d_both, act, term):
    rows, width = gate_pre.shape
    lanes, step = 128, 32
    lanes = lanes if width % lanes == 0 else width
    step = step if rows % step == 0 else rows

    def part(i, carry):
        at = pl.ds(pl.multiple_of(i * step, step), step)
        gate = gates[at, expert : expert + 1]
        total = jnp.zeros((step, lanes), F32)
        for start in range(0, width, lanes):
            cut = slice(start, start + lanes)
            pre = gate_pre[at, cut].astype(F32)
            up = up_pre[at, cut].astype(F32)
            raw = d_act[at, cut].astype(F32)
            sigmoid = 0.5 * jnp.tanh(0.5 * pre) + 0.5
            silu = pre * sigmoid
            inner = silu * up
            total = total + inner * raw
            act[at, cut] = (inner * gate).astype(BF16)
            d_inner = raw * gate
            slope = sigmoid + silu * (1.0 - sigmoid)
            d_both[at, cut] = (d_inner * up * slope).astype(BF16)
            d_both[at, width + start : width + start + lanes] = (d_inner * silu).astype(BF16)
        term[at, :] = jnp.sum(total, -1, keepdims=True)
        return carry

    lax.fori_loop(0, rows // step, part, 0)


def swiglu(expert, gate_pre, up_pre, d_act, gates):
    seq, hidden = gate_pre.shape
    rows = 256 if seq % 256 == 0 else seq
    return pl.pallas_call(
        lambda *refs: swiglu_kernel(expert, *refs),
        grid=(seq // rows,),
        in_specs=[
            pl.BlockSpec((rows, hidden), lambda i: (i, 0)),
            pl.BlockSpec((rows, hidden), lambda i: (i, 0)),
            pl.BlockSpec((rows, hidden), lambda i: (i, 0)),
            pl.BlockSpec((rows, gates.shape[1]), lambda i: (i, 0)),
        ],
        out_specs=[
            pl.BlockSpec((rows, 2 * hidden), lambda i: (i, 0)),
            pl.BlockSpec((rows, hidden), lambda i: (i, 0)),
            pl.BlockSpec((rows, 1), lambda i: (i, 0)),
        ],
        out_shape=[
            jax.ShapeDtypeStruct((seq, 2 * hidden), BF16),
            jax.ShapeDtypeStruct((seq, hidden), BF16),
            jax.ShapeDtypeStruct((seq, 1), F32),
        ],
        compiler_params=pltpu.CompilerParams(vmem_limit_bytes=48 * MIB),
        cost_estimate=pl.CostEstimate(
            flops=20 * seq * hidden, bytes_accessed=12 * seq * hidden, transcendentals=seq * hidden
        ),
    )(gate_pre, up_pre, d_act, gates)


def heads_back_kernel(d_middle, out_weight, heads_out, gates, d_heads, terms, grads, total):
    block = pl.program_id(0)
    experts, cols, _ = out_weight.shape
    rows = d_middle.shape[0]

    @pl.when(block == 0)
    def _():
        total[...] = jnp.zeros_like(total)

    lane = lax.broadcasted_iota(jnp.int32, (rows, HEAD), 1)
    table = jnp.zeros((rows, HEAD), F32)
    count = experts * (cols // HEAD)
    for expert in range(experts):
        gate = gates[:, expert : expert + 1]
        back = nt(d_middle[...], out_weight[expert])
        heads = heads_out[expert].astype(F32)
        pairing = back * heads
        for head in range(cols // HEAD):
            term = jnp.sum(pairing[:, head * HEAD : (head + 1) * HEAD], -1, keepdims=True)
            at = head * experts + expert
            table = table + jnp.where(lane == at, term, 0.0)
            table = table + jnp.where(lane == count + at, term * gate, 0.0)
        d_heads[expert] = (back * gate).astype(BF16)
        total[expert] += tn((heads * gate).astype(BF16), d_middle[...])
    terms[...] = table.T[: 2 * count]

    @pl.when(block == pl.num_programs(0) - 1)
    def _():
        _, _, chips, blocks, piece, width = grads.shape
        for chip in range(chips):
            for core in range(2):
                at = (2 * chip + core) * piece
                for j in range(blocks):
                    cut = slice(j * width, (j + 1) * width)
                    grads[core, :, chip, j] = total[:, at : at + piece, cut].astype(BF16)


def heads_back(d_middle, out_weight, heads_out, gates, chips):
    experts, seq, cols = heads_out.shape
    depth = d_middle.shape[1]
    rows = 512 if seq % 512 == 0 else seq
    count = experts * (cols // HEAD)
    split = (2, experts, chips, depth // cols, cols // chips // 2, cols)
    return pl.pallas_call(
        heads_back_kernel,
        grid=(seq // rows,),
        in_specs=[
            pl.BlockSpec((rows, depth), lambda i: (i, 0)),
            pl.BlockSpec((experts, cols, depth), lambda i: (0, 0, 0)),
            pl.BlockSpec((experts, rows, cols), lambda i: (0, i, 0)),
            pl.BlockSpec((rows, experts), lambda i: (i, 0)),
        ],
        out_specs=[
            pl.BlockSpec((experts, rows, cols), lambda i: (0, i, 0)),
            pl.BlockSpec((2 * count, rows), lambda i: (0, i)),
            pl.BlockSpec(split, lambda i: (0,) * 6),
        ],
        out_shape=[
            jax.ShapeDtypeStruct((experts, seq, cols), BF16),
            jax.ShapeDtypeStruct((2 * count, seq), F32),
            jax.ShapeDtypeStruct(split, BF16),
        ],
        scratch_shapes=[pltpu.VMEM((experts, cols, depth), F32)],
        compiler_params=pltpu.CompilerParams(vmem_limit_bytes=56 * MIB),
        cost_estimate=pl.CostEstimate(
            flops=8 * seq * depth * cols * experts // 2,
            bytes_accessed=2 * (seq * depth + 2 * experts * cols * (seq + depth)),
            transcendentals=0,
        ),
    )(d_middle, out_weight, heads_out, gates)


def lay_out_kernel(beside, core, mine, other, *outs):
    experts, piece, width = outs[-1].shape

    def lay(source):
        for kind in range(beside):
            rows_of = source[0, kind * piece : (kind + 1) * piece]
            outs[0][:, kind * width : (kind + 1) * width] = rows_of.astype(F32)
        for expert in range(experts):
            at = (beside + expert) * piece
            outs[-1][expert] = source[0, at : at + piece].astype(F32)

    pl.when(core[0] == pl.program_id(1))(lambda: lay(mine))
    pl.when(core[0] != pl.program_id(1))(lambda: lay(other))


def lay_out(core, mine, other, experts, piece, beside):
    chips, rows, width = mine.shape
    own = 2 * chips * piece
    out_specs = [pl.BlockSpec((experts, piece, width), lambda j, k: (0, 2 * j + k, 0))]
    out_shape = [jax.ShapeDtypeStruct((experts, own, width), F32)]
    if beside:
        out_specs.insert(0, pl.BlockSpec((piece, beside * width), lambda j, k: (2 * j + k, 0)))
        out_shape.insert(0, jax.ShapeDtypeStruct((own, beside * width), F32))
    return pl.pallas_call(
        lambda *refs: lay_out_kernel(beside, *refs),
        grid=(chips, 2),
        in_specs=[
            pl.BlockSpec(memory_space=pltpu.SMEM),
            pl.BlockSpec((1, rows, width), lambda j, k: (j, 0, 0)),
            pl.BlockSpec((1, rows, width), lambda j, k: (j, 0, 0)),
        ],
        out_specs=out_specs,
        out_shape=out_shape,
        compiler_params=pltpu.CompilerParams(vmem_limit_bytes=48 * MIB),
        cost_estimate=pl.CostEstimate(
            flops=0,
            bytes_accessed=4 * chips * rows * width + 4 * own * width * (beside + experts),
            transcendentals=0,
        ),
    )(core.reshape(1).astype(jnp.int32), mine, other)


def router_back(d_gates, gates):
    return gates * (d_gates - jnp.sum(gates * d_gates, -1, keepdims=True))


def tn_product(a, b):
    return mm("td,tf->df", a, b).astype(BF16)


def by_router(d_logit, router):
    columns = [(d_logit[:, e : e + 1], router[:, e].astype(F32)) for e in range(router.shape[1])]
    return sum(d * row[None, :] for d, row in columns)


def mm(spec, a, b):
    return jnp.einsum(spec, a, b, preferred_element_type=F32)


def on_device(
    hidden_in,
    segment_ids,
    attn_norm,
    attn_router,
    kv_weight,
    query_weight,
    out_weight,
    mlp_norm,
    mlp_router,
    gate_weight,
    up_weight,
    down_weight,
    cotangent,
):
    rows, width = hidden_in.shape
    count = lax.axis_size("shard")
    me = lax.axis_index("shard")
    core = lax.axis_index("core")
    seq = rows * count
    own_d = kv_weight.shape[0]
    experts = query_weight.shape[0]
    cols = query_weight.shape[2] // count
    head_count = cols // HEAD
    mlp_experts = gate_weight.shape[0]
    score_scale = HEAD ** (-0.5)

    cos, sin = rotation_tables(seq)

    small = jnp.concatenate(
        [
            attn_norm,
            mlp_norm,
            attn_router.T.reshape(-1),
            mlp_router.T.reshape(-1),
            segment_ids.astype(BF16),
        ]
    )
    small = jnp.pad(small, (0, -small.shape[0] % (16 * cols))).reshape(-1, cols)
    small_rows = small.shape[0]
    kinds = 2 + experts
    chips, chip = lax.axis_size("chip"), lax.axis_index("chip")
    owners = 2 * chips
    replica = 2 * chip + core
    piece = own_d // owners

    def columns(owner, start, size):
        at = owner * cols
        return jnp.stack(
            [lax.dynamic_slice(kv_weight, (start, at), (size, cols))]
            + [lax.dynamic_slice(kv_weight, (start, count * cols + at), (size, cols))]
            + [lax.dynamic_slice(w, (start, at), (size, cols)) for w in query_weight]
        )

    def message(owner):
        return jnp.concatenate([columns(owner, replica * piece, piece).reshape(-1, cols), small], 0)

    fetched = [swap(message(me ^ r), "shard", r) for r in range(1, count)]
    held = gather_step(gather_start(hidden_in), 0)
    joined = [jnp.concatenate([gate_weight[0], up_weight[0]], 1)]
    fetched, held, joined = together(fetched, held, joined)
    small = [small] + [rows_of[-small_rows:] for rows_of in fetched]
    fetched = jnp.stack([rows_of[:-small_rows].reshape(kinds, piece, cols) for rows_of in fetched])
    shares = lax.all_gather(fetched, REPLICAS, axis=0)
    weight = jnp.zeros((kinds, width, cols), BF16)
    weight = lax.dynamic_update_slice(weight, columns(me, 0, own_d), (0, me * own_d, 0))
    rounds = len(bit_orders(count)[0])
    for step in range(1, rounds):
        held = gather_step(held, step)
    held, weight = together(held, weight)
    small = jnp.stack([pick(small, me ^ owner) for owner in range(count)]).reshape(count, -1)
    bounds = [0]
    for size in (own_d, own_d, own_d * experts, own_d * mlp_experts, rows):
        bounds.append(bounds[-1] + size)
    pieces = [small[:, a:b] for a, b in zip(bounds, bounds[1:])]
    norm_one = pieces[0].reshape(width).astype(F32)
    norm_two = pieces[1].reshape(width).astype(F32)
    router_one = pieces[2].reshape(count, experts, own_d).transpose(0, 2, 1).reshape(width, experts)
    router_two = (
        pieces[3].reshape(count, mlp_experts, own_d).transpose(0, 2, 1).reshape(width, mlp_experts)
    )
    segments = pieces[4].reshape(seq).astype(jnp.int32)

    hidden_low = in_order(gather_end(held), me)
    hidden = hidden_low.astype(F32)
    scale_one = lax.rsqrt(jnp.mean(hidden * hidden, -1, keepdims=True) + EPSILON)
    normed = (hidden * scale_one * norm_one).astype(BF16)
    normed, cos, sin, weight, shares = together(normed, cos, sin, weight, shares)
    for r in range(1, count):
        rows_of = shares[:, r - 1].transpose(1, 0, 2, 3).reshape(kinds, own_d, cols)
        weight = lax.dynamic_update_slice(weight, rows_of, (0, (me ^ r) * own_d, 0))
    gate_one = jax.nn.softmax(jnp.dot(normed, router_one, preferred_element_type=F32), -1)
    projected = project(normed, weight, cos, sin)

    cot_ready, _ = together(cotangent, weight)
    wide_cot = lax.all_gather(cot_ready, "shard", axis=0, tiled=True)
    heads_out, stats = attend(projected, segments)
    heads_out, wide_cot = together(heads_out, wide_cot)
    for expert in range(experts):
        weighted = gate_one[:, expert : expert + 1] * jnp.dot(
            heads_out[expert], out_weight[expert], preferred_element_type=F32
        )
        attn_mix = weighted if expert == 0 else attn_mix + weighted
    own_hidden = hidden_in.astype(F32)
    attn_mix, wide_cot = together(attn_mix.astype(BF16), wide_cot)
    d_act = [mm("td,fd->tf", wide_cot, down_weight[0]).astype(BF16)]
    joined += [jnp.concatenate(both, 1) for both in zip(gate_weight[1:], up_weight[1:])]
    attn_sum, ((wide_cot, d_act), joined) = scatter_sum(
        by_distance(attn_mix, me, count), [(wide_cot, d_act), joined]
    )
    middle = own_hidden + attn_sum
    scale_two = lax.rsqrt(jnp.mean(middle * middle, -1, keepdims=True) + EPSILON)
    normed_two = (middle * scale_two * norm_two).astype(BF16)

    for expert in range(1, mlp_experts):
        d_act.append(mm("td,fd->tf", wide_cot, down_weight[expert]).astype(BF16))
    held = gather_start(normed_two)
    for step in range(rounds):
        held = gather_step(held, step)
    held, d_act = together(held, d_act)
    wide_normed = in_order(gather_end(held), me, hidden_low)
    wide_gate = jax.nn.softmax(jnp.dot(wide_normed, router_two, preferred_element_type=F32), -1)
    d_both = []
    acts = []
    gate_terms = []
    expert_grads = []
    for expert in range(mlp_experts):
        gate_pre = mm("td,df->tf", wide_normed, gate_weight[expert]).astype(BF16)
        up_pre = mm("td,df->tf", wide_normed, up_weight[expert]).astype(BF16)
        both, act, term = swiglu(expert, gate_pre, up_pre, d_act[expert], wide_gate)
        if expert == 0:
            grads = mm("tf,td->fd", both, wide_normed).astype(BF16)
            grads, wide_normed = together(grads, wide_normed)
            expert_grads.append(replica_scatter(grads.reshape(2, -1, width)))
        d_both.append(both)
        acts.append(act)
        gate_terms.append(term)
    d_logit_two = router_back(jnp.concatenate(gate_terms, -1), wide_gate)
    wide_grad = sum(mm("tf,df->td", d, w) for d, w in zip(d_both, joined))
    wide_grad = (wide_grad + by_router(d_logit_two, router_two)).astype(BF16)
    wide_grad, d_both = together(wide_grad, d_both)
    late_grads = [mm("tf,td->fd", d, wide_normed).astype(BF16) for d in d_both[1:]]
    d_normed_two, (late_grads,) = scatter_sum(by_distance(wide_grad, me, count), [late_grads])
    expert_grads += [replica_scatter(grads.reshape(2, -1, width)) for grads in late_grads]
    d_normed_two, acts, expert_grads[0] = together(d_normed_two, acts, expert_grads[0])
    acts = jnp.concatenate(acts, 1)
    down_grads = mm("tf,td->fd", acts, wide_cot).astype(BF16).reshape(mlp_experts, -1, width)

    def own_rows(whole):
        return lax.dynamic_slice_in_dim(whole, me * rows, rows, 0)

    d_norm_two = jnp.sum(d_normed_two * middle * scale_two, 0)
    d_middle = norm_back(d_normed_two, middle, scale_two, norm_two) + cotangent.astype(F32)

    d_router_two = jnp.dot(wide_normed.astype(F32).T, d_logit_two, precision=HIGHEST)
    held = gather_start(d_middle.astype(BF16))
    for step in range(rounds):
        held = gather_step(held, step)
        if step == 0:
            held, down_grads, acts, d_router_two = together(held, down_grads, acts, d_router_two)
            partial_mix = mm("tf,fd->td", acts, down_weight.reshape(-1, width)).astype(BF16)
    mix_cut = scatter_cut(scatter_start(by_distance(partial_mix, me, count)), 0)
    mix_sent, held = together([sent for _, sent in mix_cut], held)
    mix_cut = [(kept, sent) for (kept, _), sent in zip(mix_cut, mix_sent)]
    wide_middle = in_order(gather_end(held), me, wide_normed)
    down_grads = replica_scatter(down_grads)
    d_heads, terms, out_grad = heads_back(wide_middle, out_weight, heads_out, gate_one, chips)
    mix_sent, d_heads, terms, out_grad = together(mix_sent, d_heads, terms, out_grad)
    mix_cut = [(kept, sent) for (kept, _), sent in zip(mix_cut, mix_sent)]
    out_kept, out_got = chip_sum(out_grad, 0)
    mix_pairs = scatter_send(mix_cut, 0)
    raw_terms, delta = terms.reshape(2, head_count, experts, seq)
    d_projected = attend_back(projected, segments, cos, sin, d_heads, stats, delta)
    mix_pairs, d_projected, expert_grads, out_got = arrived(
        mix_pairs, d_projected, expert_grads, out_got
    )
    mix_held = scatter_add(mix_pairs)
    mix_pairs = scatter_step(mix_held, 1) if rounds > 1 else []
    chip_rounds = chips.bit_length() - 1
    grads = [
        tn_product(normed, d_projected[k]).reshape(count, chips, 2, piece, cols) for k in range(kinds)
    ]
    kept = [lax.dynamic_index_in_dim(g, core, 2, keepdims=False) for g in grads]
    sent = jnp.stack([lax.dynamic_index_in_dim(g, 1 - core, 2, keepdims=False) for g in grads])
    sent, d_projected = together(sent, d_projected)
    got = swap(sent, "core", 1)
    d_logit_one = router_back(jnp.sum(raw_terms, 0).T, gate_one)
    share = mm("ktf,kdf->td", d_projected, weight) + by_router(d_logit_one, router_one)
    mix_pairs, share, got = arrived(mix_pairs, share.astype(BF16), got)
    pair = [add_low(one, new) for one, new in zip(kept, got)]
    out_pair = add_low(out_kept, out_got)

    def piece_of(owner):
        parts = [lax.dynamic_index_in_dim(one, owner, 1, keepdims=False) for one in pair]
        parts.append(lax.dynamic_index_in_dim(out_pair, owner, 1, keepdims=False))
        return jnp.concatenate([part.reshape(-1, cols) for part in parts], 0)

    held = scatter_start([piece_of(chip ^ r) for r in range(chips)], "chip")
    pairs = scatter_step(held, 0, "chip") if chip_rounds else []
    came = [got for _, got in pairs]
    d_normed, ((came, down_grads),) = scatter_sum(
        by_distance(share, me, count), [(came, down_grads)]
    )
    pairs = [(kept, got) for (kept, _), got in zip(pairs, came)]
    if chip_rounds:
        pairs, d_logit_one = arrived(pairs, d_logit_one)
    held = scatter_add(pairs) if chip_rounds else held
    own_scale = own_rows(scale_one)
    d_norm_one = jnp.sum(d_normed * own_hidden * own_scale, 0)
    d_router_one = jnp.dot(normed.astype(F32).T, d_logit_one, precision=HIGHEST)
    for step in range(1, chip_rounds):
        pairs = scatter_step(held, step, "chip")
        if step == 1:
            pairs, d_router_one, d_norm_one = arrived(pairs, d_router_one, d_norm_one)
        held = scatter_add(pairs)
    own = scatter_end(held).astype(BF16)
    own, out_own = jnp.split(own, [kinds * count * piece], 0)
    own = own.reshape(kinds, count, piece, cols)
    out_own = out_own.reshape(experts, count, piece, cols)
    input_grad = norm_back(d_normed, own_hidden, own_scale, norm_one) + d_middle

    parts = [lax.dynamic_index_in_dim(own, me ^ r, 1, keepdims=False) for r in range(count)]
    parts = [parts[0]] + [swap(parts[r], "shard", r) for r in range(1, count)]
    own = jnp.concatenate([pick(parts, me ^ owner) for owner in range(count)], -1)
    out_own = jnp.concatenate([out_own[:, owner] for owner in range(count)], -1)
    own = own.reshape(-1, width)
    grain = 16 * len(bit_orders(chips))
    out_own = out_own.reshape(-1, width)
    out_own = jnp.pad(out_own, ((0, -out_own.shape[0] % grain), (0, 0)))
    out_held = gather_start(out_own, "chip")
    for step in range(chip_rounds):
        out_held = gather_step(out_held, step, "chip")
    own, out_held = together(own, out_held)
    out_whole = in_order(gather_end(out_held), chip)
    out_other = swap(out_whole, "core", 1)
    out_whole, out_other = [both.reshape(chips, -1, width) for both in (out_whole, out_other)]
    (out_grad,) = lay_out(core, out_whole, out_other, experts, piece, 0)
    sums = jnp.concatenate([d_norm_one[None], d_norm_two[None], d_router_one.T, d_router_two.T], 0)
    sums = scatter_small(
        [lax.dynamic_slice_in_dim(sums, (me ^ r) * own_d, own_d, 1) for r in range(count)]
    )
    high = sums.astype(BF16)
    ride = jnp.stack([high, (sums - high.astype(F32)).astype(BF16)]).reshape(-1)
    own_rows_count = own.shape[0]
    ride_rows = -(-ride.shape[0] // width)
    ride_rows += -(own_rows_count + ride_rows) % grain
    ride = jnp.pad(ride, (0, ride_rows * width - ride.shape[0])).reshape(ride_rows, width)
    own = jnp.concatenate([own, ride], 0)
    gate_grads, up_grads = [
        jnp.stack([grads[kind] for grads in expert_grads]).astype(F32).transpose(0, 2, 1)
        for kind in range(2)
    ]
    down_grads = down_grads.astype(F32)
    own, gate_grads, up_grads, down_grads = together(own, gate_grads, up_grads, down_grads)
    held = gather_start(own, "chip")
    for step in range(chip_rounds):
        held = gather_step(held, step, "chip")
    mix_held = scatter_add(mix_pairs) if mix_pairs else mix_held
    for step in range(2, rounds):
        mix_held = scatter_add(scatter_step(mix_held, step))
    output = (middle + scatter_end(mix_held)).astype(BF16)
    held, out_grad = together(held, out_grad)
    whole = in_order(gather_end(held), chip)
    other = swap(whole, "core", 1)
    whole, other = [both.reshape(chips, -1, width) for both in (whole, other)]
    rides = jnp.concatenate([whole[:, own_rows_count:], other[:, own_rows_count:]], 0)
    rides = rides.reshape(owners, -1)[:, : 2 * sums.size].astype(F32)
    sums = jnp.sum(rides.reshape(2 * owners, -1), 0).reshape(sums.shape)
    kv_grad, query_grad = lay_out(core, whole, other, experts, piece, 2)
    return (
        output,
        input_grad,
        sums[0],
        sums[2 : 2 + experts].T,
        kv_grad,
        query_grad,
        out_grad,
        sums[1],
        sums[2 + experts :].T,
        gate_grads,
        up_grads,
        down_grads,
    )


def solution(mesh):
    devices = mesh.devices
    mesh = Mesh(devices.reshape(-1, 2, devices.shape[1]), ("chip", "core", "shard"))
    return jax.shard_map(
        on_device,
        mesh=mesh,
        in_specs=(
            P(("chip", "core", "shard"), None),
            P(("chip", "core", "shard")),
            P("shard"),
            P("shard", None),
            P("shard", None),
            P(None, "shard", None),
            P(None, "shard", None),
            P("shard"),
            P("shard", None),
            P(None, None, "shard"),
            P(None, None, "shard"),
            P(None, "shard", None),
            P(("chip", "core", "shard"), None),
        ),
        out_specs=(
            P(("chip", "core", "shard"), None),
            P(("chip", "core", "shard"), None),
            P("shard"),
            P("shard", None),
            P("shard", None),
            P(None, "shard", None),
            P(None, "shard", None),
            P("shard"),
            P("shard", None),
            P(None, None, ("shard", "chip", "core")),
            P(None, None, ("shard", "chip", "core")),
            P(None, ("shard", "chip", "core"), None),
        ),
        check_vma=False,
    )
```

time: 2940 us -> 1060 us (0.36)
  waiting for transfers between devices: 1860 us -> 283 us
  matrix products: 659 us -> 307 us
  Pallas kernels: 0 us -> 166 us
  blocking collectives: 65.1 us -> 0 us
  other arithmetic: 178 us -> 122 us
  starting transfers between devices: 27.4 us -> 65.8 us
  local copies, waits for them, and re-layouts: 125 us -> 92.5 us
    all_gather x10 -> x2, waiting for transfers between devices: 691 us -> 9.33 us  [the longest x1 9.33 us: on_device(): shares = lax.all_gather(fetched, REPLICAS, axis=0)]
    psum x1 -> x0, waiting for transfers between devices: 669 us -> none  [on_device(): lax.psum(share_query.astype(jnp.bfloat16), 'rep').astype(jnp.float32)]
    dot_general x47 -> x23, matrix products: 618 us -> 307 us  [the longest x17 273 us: mm(): return jnp.einsum(spec, a, b, preferred_element_type=F32)]
    reduce_scatter x3, waiting for transfers between devices: 308 us -> 0.04 us  [replica_scatter(): return lax.psum_scatter(whole, REPLICAS, scatter_dimension=1, tiled=True)]
    pallas_call x0 -> x8, Pallas kernels: none -> 166 us  [the longest x1 42 us: attend_back(): pl.pallas_call(lambda *refs: attend_back_kernel(experts, blocks, *refs),...]
    ppermute x12 -> x63, waiting for transfers between devices: 155 us -> 273 us  [swap(): return lax.ppermute(value, axis, [(i, i ^ bits) for i in range(count)])]
    convert_element_type x18 -> x15, other arithmetic: 94.4 us -> 33.8 us  [the longest x6 11.7 us: scatter_cut(): have[r ^ bit].astype(BF16)]
    another operation x13 -> x11, other arithmetic: 58.5 us -> 6.33 us
  transfers between devices with their start and end apart: 29 -> 68, of which waited for: 17 -> 30; matrix products, arithmetic and copies ran while one was open for 25% -> 38% of each run, Pallas kernels for 0% -> 14%
where the time goes in v1:
time: 1060 us; the launch traced here: 1050 us
  matrix products  307 us (29%)
  waiting for transfers between devices  283 us (27%)
  Pallas kernels  166 us (16%)
  other arithmetic  122 us (12%)
  local copies, waits for them, and re-layouts  92.5 us (9%)
  starting transfers between devices  65.8 us (6%)
  between operations  16.3 us (2%)
    ppermute x63, waiting for transfers between devices, swap(): return lax.ppermute(value, axis, [(i, i ^ bits) for i in range(count)])  273 us
    dot_general x17, matrix products, mm(): return jnp.einsum(spec, a, b, preferred_element_type=F32)  273 us
    ppermute x63, starting transfers between devices, swap(): return lax.ppermute(value, axis, [(i, i ^ bits) for i in range(count)])  65.2 us
    pallas_call x1, Pallas kernels, attend_back(): pl.pallas_call(lambda *refs: attend_back_kernel(experts, blocks, *refs),...  42 us
    pallas_call x1, Pallas kernels, attend(): pl.pallas_call(lambda *refs: attend_kernel(experts, blocks, *refs), grid=...  37.8 us
    unnamed x233, local copies, waits for them, and re-layouts  28.7 us
    pallas_call x2, Pallas kernels, swiglu(): pl.pallas_call(lambda *refs: swiglu_kernel(expert, *refs), grid=(seq // r...  25.1 us
    pallas_call x1, Pallas kernels, heads_back(): pl.pallas_call(heads_back_kernel, grid=(seq // rows,), in_specs=[pl.Block...  22.8 us
  transfers between devices with their start and end apart: 68, of which 30 were waited for; matrix products, arithmetic and copies ran while one was open for 38% of the time, Pallas kernels for 14%

profile of v1, /device:TPU:0, one launch (start us, length us, event | category | flops | bytes accessed | tf_op | source)
XLA Modules:
  0.0 1052.5 jit_solution(13883589835994585744)
XLA Ops:
  24.4 13.1 %slice_bitcast_fusion = (bf16[2048,1408]{1,0:T(8,128)(2,1)}, bf16[2048,1408]{1,0:T(8,128)(2,1)S(1)}, bf16[2048,1408]{1,0:T(8,128)(2,1)S(1)}, bf16[2048,1408]{1,0:T(8,128)(2,1)}) fusion(bf16[2,2048,1408]{2,1,0:T(8,128)(2,1)} %param.23, bf16[2,2048,1408]{2,1,0:T(8,128)(2,1)} %param.22), kind=kLoop, calls=%fused_computation.24 | loop fusion | bytes 46137344 | tf_op jit(solution)/shard_map/unstack | solution.py:720
  71.8 14.5 %collective-permute-done.6 = bf16[192,2048]{1,0:T(8,128)(2,1)} collective-permute-done((bf16[192,2048]{1,0:T(8,128)(2,1)}, bf16[192,2048]{1,0:T(8,128)(2,1)}, u32[]{:S(2)}, u32[]{:S(2)}) %collective-permute-start.6) | collective-permute-done | bytes 786464 | tf_op jit(solution)/shard_map/ppermute | solution.py:22
  128.4 21.3 %shard_map.220.refs_2_.refs_3_.refs_4_.refs_5_.refs_6_.refs_7_ = bf16[4,1536,512]{2,1,0:T(8,128)(2,1)} custom-call(bf16[1536,2048]{1,0:T(8,128)(2,1)} %fusion.2.normed, bf16[4,2048,512]{2,1,0:T(8,128)(2,1)} %constant_dynamic-update-slice_fusion.weight, f32[1536,128]{1,0:T(8,128)S(1)} %get-tuple-element.200.cos.refs_2_, ...), custom_call_target="tpu_custom_call" | custom-call | flops 12884901888 | bytes 20971520 | tf_op jit(solution)/shard_map/pallas_call | solution.py:213
  149.7 37.8 %shard_map.221 = (bf16[2,1536,512]{2,1,0:T(8,128)(2,1)S(1)}, f32[4,2,1536]{2,1,0:T(2,128)S(1)}) custom-call(s32[1536,1]{1,0:T(8,128)S(1)} %bitcast.325, s32[1,1536]{1,0:T(1,128)S(1)} %bitcast.328, bf16[4,1536,512]{2,1,0:T(8,128)(2,1)} %shard_map.220.refs_2_.refs_3_.refs_4_.refs_5_.refs_6_.refs_7_, ...), custom_call_target="tpu_custom_call" | custom-call | flops 10737418240 | bytes 9437184 | tf_op jit(solution)/shard_map/pallas_call | solution.py:289
  212.9 15.1 %convolution_convert_fusion.9.refs_2_ = bf16[1536,1408]{1,0:T(8,128)(2,1)} fusion(bf16[1536,2048]{1,0:T(8,128)(2,1)} %all-gather.4.cloned.1.call-done, bf16[2,1408,2048]{2,1,0:T(8,128)(2,1)} %param.24), kind=kOutput, calls=%fused_computation.20 | convolution fusion | flops 8860532736 | bytes 16384000 | tf_op jit(solution)/shard_map/td,fd->tf/dot_general | solution.py:611
  228.0 18.6 %collective-permute-done.9 = bf16[384,2048]{1,0:T(8,128)(2,1)S(1)} collective-permute-done((bf16[384,2048]{1,0:T(8,128)(2,1)}, bf16[384,2048]{1,0:T(8,128)(2,1)S(1)}, u32[]{:S(2)}, u32[]{:S(2)}) %collective-permute-start.9) | collective-permute-done | bytes 1572896 | tf_op jit(solution)/shard_map/ppermute | solution.py:22
  255.9 11.2 %collective-permute-done.11 = bf16[192,2048]{1,0:T(8,128)(2,1)S(1)} collective-permute-done((bf16[192,2048]{1,0:T(8,128)(2,1)S(1)}, bf16[192,2048]{1,0:T(8,128)(2,1)S(1)}, u32[]{:S(2)}, u32[]{:S(2)}) %collective-permute-start.11) | collective-permute-done | bytes 786464 | tf_op jit(solution)/shard_map/ppermute | solution.py:22
  276.5 16.3 %collective-permute-done.13 = bf16[192,2048]{1,0:T(8,128)(2,1)S(1)} collective-permute-done((bf16[192,2048]{1,0:T(8,128)(2,1)S(1)}, bf16[192,2048]{1,0:T(8,128)(2,1)S(1)}, u32[]{:S(2)}, u32[]{:S(2)}) %collective-permute-start.13) | collective-permute-done | bytes 786464 | tf_op jit(solution)/shard_map/ppermute | solution.py:22
  294.8 15.1 %convolution_convert_fusion.8.refs_2_ = bf16[1536,1408]{1,0:T(8,128)(2,1)} fusion(bf16[1536,2048]{1,0:T(8,128)(2,1)} %all-gather.4.cloned.1.call-done, bf16[2,1408,2048]{2,1,0:T(8,128)(2,1)} %param.24), kind=kOutput, calls=%fused_computation.19 | convolution fusion | flops 8860532736 | bytes 16384000 | tf_op jit(solution)/shard_map/td,fd->tf/dot_general | solution.py:611
  310.2 13.5 %collective-permute-done.15 = bf16[192,2048]{1,0:T(8,128)(2,1)} collective-permute-done((bf16[192,2048]{1,0:T(8,128)(2,1)S(1)}, bf16[192,2048]{1,0:T(8,128)(2,1)}, u32[]{:S(2)}, u32[]{:S(2)}) %collective-permute-start.15) | collective-permute-done | bytes 786464 | tf_op jit(solution)/shard_map/ppermute | solution.py:22
  326.1 11.4 %convolution_convert_fusion.6.refs_1_ = bf16[1536,1408]{1,0:T(8,128)(2,1)} fusion(bf16[1536,2048]{1,0:T(8,128)(2,1)S(1)} %maximum_dynamic-update-slice_fusion.8, bf16[2,2048,1408]{2,1,0:T(8,128)(2,1)S(1)} %bitcast.344), kind=kOutput, calls=%fused_computation.17 | convolution fusion | flops 8860532736 | bytes 16384000 | tf_op jit(solution)/shard_map/td,df->tf/dot_general | solution.py:611
  337.5 13.7 %convolution_convert_fusion.7.refs_0_ = bf16[1536,1408]{1,0:T(8,128)(2,1)} fusion(bf16[1536,2048]{1,0:T(8,128)(2,1)S(1)} %maximum_dynamic-update-slice_fusion.8, bf16[2,2048,1408]{2,1,0:T(8,128)(2,1)} %param.22), kind=kOutput, calls=%fused_computation.18 | convolution fusion | flops 8860532736 | bytes 16384000 | tf_op jit(solution)/shard_map/td,df->tf/dot_general | solution.py:611
  354.3 12.6 %shard_map.222 = (bf16[1536,2816]{1,0:T(8,128)(2,1)}, bf16[1536,1408]{1,0:T(8,128)(2,1)S(1)}, f32[1536,1]{1,0:T(8,128)S(1)}) custom-call(bf16[1536,1408]{1,0:T(8,128)(2,1)} %convolution_convert_fusion.7.refs_0_, bf16[1536,1408]{1,0:T(8,128)(2,1)} %convolution_convert_fusion.6.refs_1_, bf16[1536,1408]{1,0:T(8,128)(2,1)} %convolution_convert_fusion.9.refs_2_, ...), custom_call_target="tpu_custom_call" | custom-call | flops 43253760 | bytes 25952256 | tf_op jit(solution)/shard_map/pallas_call | solution.py:457
  367.0 25.5 %convolution_convert_fusion.2 = bf16[2816,2048]{1,0:T(8,128)(2,1)} fusion(bf16[1536,2816]{1,0:T(8,128)(2,1)} %get-tuple-element.230, bf16[1536,2048]{1,0:T(8,128)(2,1)S(1)} %bitcast.333), kind=kOutput, calls=%fused_computation.13 | convolution fusion | flops 17722507264 | bytes 26476544 | tf_op jit(solution)/shard_map/tf,td->fd/dot_general | solution.py:611
  392.8 15.4 %convolution_convert_fusion.4.refs_1_ = bf16[1536,1408]{1,0:T(8,128)(2,1)} fusion(bf16[1536,2048]{1,0:T(8,128)(2,1)} %copy-done.14, bf16[2,2048,1408]{2,1,0:T(8,128)(2,1)} %param.23), kind=kOutput, calls=%fused_computation.15 | convolution fusion | flops 8860532736 | bytes 16384000 | tf_op jit(solution)/shard_map/td,df->tf/dot_general | solution.py:611
  408.3 15.1 %convolution_convert_fusion.5.refs_0_ = bf16[1536,1408]{1,0:T(8,128)(2,1)} fusion(bf16[1536,2048]{1,0:T(8,128)(2,1)} %copy-done.14, bf16[2,2048,1408]{2,1,0:T(8,128)(2,1)} %param.22), kind=kOutput, calls=%fused_computation.16 | convolution fusion | flops 8860532736 | bytes 16384000 | tf_op jit(solution)/shard_map/td,df->tf/dot_general | solution.py:611
  423.4 12.4 %shard_map.223 = (bf16[1536,2816]{1,0:T(8,128)(2,1)}, bf16[1536,1408]{1,0:T(8,128)(2,1)S(1)}, f32[1536,1]{1,0:T(8,128)S(1)}) custom-call(bf16[1536,1408]{1,0:T(8,128)(2,1)} %convolution_convert_fusion.5.refs_0_, bf16[1536,1408]{1,0:T(8,128)(2,1)} %convolution_convert_fusion.4.refs_1_, bf16[1536,1408]{1,0:T(8,128)(2,1)} %convolution_convert_fusion.8.refs_2_, ...), custom_call_target="tpu_custom_call" | custom-call | flops 43253760 | bytes 25952256 | tf_op jit(solution)/shard_map/pallas_call | solution.py:457
  440.7 24.9 %fusion.73 = f32[1536,2048]{1,0:T(8,128)} fusion(bf16[1536,2816]{1,0:T(8,128)(2,1)} %get-tuple-element.241, bf16[2048,2816]{1,0:T(8,128)(2,1)} %pad_maximum_fusion.1), kind=kOutput, calls=%fused_computation.313 | convolution fusion | flops 17716740096 | bytes 32768000 | tf_op jit(solution)/shard_map/tf,df->td/dot_general | solution.py:611
  465.6 26.7 %add_convert_fusion = bf16[1536,2048]{1,0:T(8,128)(2,1)} fusion(f32[1536,2048]{1,0:T(8,128)} %fusion.73, bf16[1536,2816]{1,0:T(8,128)(2,1)} %get-tuple-element.230, bf16[2048,2816]{1,0:T(8,128)(2,1)} %pad_maximum_fusion, f32[2048]{0:T(1024)S(1)} %bitcast.423, f32[1536]{0:T(1024)S(1)} %get-tuple-element.353, f32[2048]{0:T(1024)S(1)} %bitcast.422, ...), kind=kOutput, calls=%fused_computation.7 | convolution fusion | flops 17735614464 | bytes 39088128 | tf_op jit(solution)/shard_map/tf,df->td/dot_general | solution.py:611
  496.6 24.7 %convolution_convert_fusion.1 = bf16[2816,2048]{1,0:T(8,128)(2,1)} fusion(bf16[1536,2816]{1,0:T(8,128)(2,1)} %get-tuple-element.241, bf16[1536,2048]{1,0:T(8,128)(2,1)} %copy-done.14), kind=kOutput, calls=%fused_computation.12 | convolution fusion | flops 17722507264 | bytes 26476544 | tf_op jit(solution)/shard_map/tf,td->fd/dot_general | solution.py:611
  566.5 21.1 %convolution_convert_fusion = bf16[2816,2048]{1,0:T(8,128)(2,1)} fusion(bf16[1536,2816]{1,0:T(8,128)(2,1)S(1)} %constant_dynamic-update-slice_fusion.3, bf16[1536,2048]{1,0:T(8,128)(2,1)S(1)} %bitcast.430), kind=kOutput, calls=%fused_computation.11 | convolution fusion | flops 17722507264 | bytes 26476544 | tf_op jit(solution)/shard_map/tf,td->fd/dot_general | solution.py:611
  592.6 23.6 %convolution_convert_fusion.3 = bf16[1536,2048]{1,0:T(8,128)(2,1)S(1)} fusion(bf16[1536,2816]{1,0:T(8,128)(2,1)} %copy-done.34, bf16[2816,2048]{1,0:T(8,128)(2,1)} %bitcast.428), kind=kOutput, calls=%fused_computation.14 | convolution fusion | flops 17719885824 | bytes 26476544 | tf_op jit(solution)/shard_map/tf,fd->td/dot_general | solution.py:611
  630.4 22.8 %shard_map.224 = (bf16[2,1536,512]{2,1,0:T(8,128)(2,1)}, f32[16,1536]{1,0:T(8,128)}, bf16[2,2,4,4,64,512]{5,4,3,2,1,0:T(8,128)(2,1)}) custom-call(bf16[1536,2048]{1,0:T(8,128)(2,1)} %maximum_dynamic-update-slice_fusion.12.d_middle, bf16[2,512,2048]{2,1,0:T(8,128)(2,1)} %out_weight.1, bf16[2,1536,512]{2,1,0:T(8,128)(2,1)} %copy-done.10, f32[1536,2]{1,0:T(8,128)} %copy-done.27), custom_call_target="tpu_custom_call" | custom-call | flops 12884901888 | bytes 20971520 | tf_op jit(solution)/shard_map/pallas_call | solution.py:526
  662.5 42.0 %shard_map.225 = bf16[4,1536,512]{2,1,0:T(8,128)(2,1)} custom-call(s32[1,1536]{1,0:T(1,128)S(1)} %bitcast.329, s32[1536,1]{1,0:T(8,128)S(1)} %bitcast.326, f32[1536,128]{1,0:T(8,128)S(1)} %copy-done.7, f32[1536,128]{1,0:T(8,128)S(1)} %get-tuple-element.201.sin.refs_3_, bf16[4,1536,512]{2,1,0:T(8,128)(2,1)} %shard_map.220.refs_2_.refs_3_.refs_4_.refs_5_.refs_6_.refs_7_, ...), custom_call_target="tpu_custom_call" | custom-call | flops 26843545600 | bytes 15728640 | tf_op jit(solution)/shard_map/pallas_call | solution.py:375
  737.2 18.9 %fusion.3 = bf16[1536,2048]{1,0:T(8,128)(2,1)S(1)} fusion(bf16[4,1536,512]{2,1,0:T(8,128)(2,1)} %shard_map.225, bf16[4,2048,512]{2,1,0:T(8,128)(2,1)} %constant_dynamic-update-slice_fusion.weight, f32[2048]{0:T(1024)S(1)} %bitcast.421, f32[1536]{0:T(1024)S(1)} %get-tuple-element.351, f32[2048]{0:T(1024)S(1)} %bitcast.420, f32[1536]{0:T(1024)S(1)} %get-tuple-element.350), kind=kOutput, calls=%fused_computation.6 | convolution fusion | flops 12900630528 | bytes 21000192 | tf_op jit(solution)/shard_map/ktf,kdf->td/dot_general | solution.py:611
  787.8 58.2 %collective-permute-done.37 = bf16[1536,512]{1,0:T(8,128)(2,1)} collective-permute-done((bf16[1536,512]{1,0:T(8,128)(2,1)}, bf16[1536,512]{1,0:T(8,128)(2,1)}, u32[]{:S(2)}, u32[]{:S(2)}) %collective-permute-start.37) | collective-permute-done | bytes 1572896 | tf_op jit(solution)/shard_map/ppermute | solution.py:22
  872.3 14.7 %collective-permute-done.41 = bf16[768,512]{1,0:T(8,128)(2,1)S(1)} collective-permute-done((bf16[768,512]{1,0:T(8,128)(2,1)S(1)}, bf16[768,512]{1,0:T(8,128)(2,1)S(1)}, u32[]{:S(2)}, u32[]{:S(2)}) %collective-permute-start.41) | collective-permute-done | bytes 786464 | tf_op jit(solution)/shard_map/ppermute | solution.py:22
  935.9 23.7 %collective-permute-done.55 = bf16[144,2048]{1,0:T(8,128)(2,1)} collective-permute-done((bf16[144,2048]{1,0:T(8,128)(2,1)S(1)}, bf16[144,2048]{1,0:T(8,128)(2,1)}, u32[]{:S(2)}, u32[]{:S(2)}) %collective-permute-start.55) | collective-permute-done | bytes 589856 | tf_op jit(solution)/shard_map/ppermute | solution.py:22
  959.6 14.9 %collective-permute-done.59 = bf16[144,2048]{1,0:T(8,128)(2,1)} collective-permute-done((bf16[144,2048]{1,0:T(8,128)(2,1)S(1)}, bf16[144,2048]{1,0:T(8,128)(2,1)}, u32[]{:S(2)}, u32[]{:S(2)}) %collective-permute-start.59) | collective-permute-done | bytes 589856 | tf_op jit(solution)/shard_map/ppermute | solution.py:22
  981.6 18.2 %collective-permute-done.56 = bf16[144,2048]{1,0:T(8,128)(2,1)} collective-permute-done((bf16[144,2048]{1,0:T(8,128)(2,1)S(1)}, bf16[144,2048]{1,0:T(8,128)(2,1)}, u32[]{:S(2)}, u32[]{:S(2)}) %collective-permute-start.56) | collective-permute-done | bytes 589856 | tf_op jit(solution)/shard_map/ppermute | solution.py:22
  999.9 12.2 %collective-permute-done.57 = bf16[144,2048]{1,0:T(8,128)(2,1)} collective-permute-done((bf16[144,2048]{1,0:T(8,128)(2,1)}, bf16[144,2048]{1,0:T(8,128)(2,1)}, u32[]{:S(2)}, u32[]{:S(2)}) %collective-permute-start.57) | collective-permute-done | bytes 589856 | tf_op jit(solution)/shard_map/ppermute | solution.py:22
  1034.2 10.4 shard_map.227
  (560 shorter events, 396.6 us)
Async XLA Ops:
  7.2 103.3 %all-gather.6.cloned.1.call-start = ((), (), s32[]{:S(2)}) async-start(), calls=%async_computation.7 | async-start | bytes 7077888 | tf_op jit(solution)/shard_map/all_gather | solution.py:677
  9.7 33.9 %collective-permute-start.3 = (bf16[192,2048]{1,0:T(8,128)(2,1)}, bf16[192,2048]{1,0:T(8,128)(2,1)}, u32[]{:S(2)}, u32[]{:S(2)}) collective-permute-start(bf16[192,2048]{1,0:T(8,128)(2,1)} %get-tuple-element.185), channel_id=1, source_target_pairs={{0,1},{1,0},{2,3},{3,2},{4,5},{5,4},{6,7},{7,6},{8,9},{9,8},{10,11... | collective-permute-start | bytes 2359304 | tf_op jit(solution)/shard_map/ppermute | solution.py:22
  45.3 143.8 %all-gather.4.cloned.1.call-start = ((), (), s32[]{:S(2)}) async-start(), calls=%async_computation.3 | async-start | bytes 7864320 | tf_op jit(solution)/shard_map/all_gather | solution.py:709
  52.5 33.7 %collective-permute-start.6 = (bf16[192,2048]{1,0:T(8,128)(2,1)}, bf16[192,2048]{1,0:T(8,128)(2,1)}, u32[]{:S(2)}, u32[]{:S(2)}) collective-permute-start(bf16[192,2048]{1,0:T(8,128)(2,1)} %collective-permute-done.3), channel_id=1, source_target_pairs={{0,2},{1,3},{2,0},{3,1},{4,6},{5,7},{6,4},{7,5},{8,10},{9,11},{10,... | collective-permute-start | bytes 2359304 | tf_op jit(solution)/shard_map/ppermute | solution.py:22
  53.0 33.2 %collective-permute-start.7 = (bf16[192,2048]{1,0:T(8,128)(2,1)S(1)}, bf16[192,2048]{1,0:T(8,128)(2,1)}, u32[]{:S(2)}, u32[]{:S(2)}) collective-permute-start(bf16[192,2048]{1,0:T(8,128)(2,1)S(1)} %get-tuple-element.186), channel_id=1, source_target_pairs={{0,1},{1,0},{2,3},{3,2},{4,5},{5,4},{6,7},{7,6},{8,9},{9,8},{10,11... | collective-permute-start | bytes 2359304 | tf_op jit(solution)/shard_map/ppermute | solution.py:22
  53.5 34.0 %collective-permute-start.8 = (bf16[192,2048]{1,0:T(8,128)(2,1)}, bf16[192,2048]{1,0:T(8,128)(2,1)}, u32[]{:S(2)}, u32[]{:S(2)}) collective-permute-start(bf16[192,2048]{1,0:T(8,128)(2,1)} %collective-permute-done.4), channel_id=1, source_target_pairs={{0,1},{1,0},{2,3},{3,2},{4,5},{5,4},{6,7},{7,6},{8,9},{9,8},{10,11... | collective-permute-start | bytes 2359304 | tf_op jit(solution)/shard_map/ppermute | solution.py:22
  119.3 432.0 %reduce-scatter.4.cloned.1.call-start = ((), (), s32[]{:S(2)}) async-start(), calls=%async_computation.4 | async-start | bytes 12976128 | tf_op jit(solution)/shard_map/reduce_scatter | solution.py:132
  209.8 36.8 %collective-permute-start.9 = (bf16[384,2048]{1,0:T(8,128)(2,1)}, bf16[384,2048]{1,0:T(8,128)(2,1)S(1)}, u32[]{:S(2)}, u32[]{:S(2)}) collective-permute-start(bf16[384,2048]{1,0:T(8,128)(2,1)} %pad_maximum_fusion.5), channel_id=1, source_target_pairs={{0,2},{1,3},{2,0},{3,1},{4,6},{5,7},{6,4},{7,5},{8,10},{9,11},{10,... | collective-permute-start | bytes 4718600 | tf_op jit(solution)/shard_map/ppermute | solution.py:22
  211.4 36.4 %collective-permute-start.10 = (bf16[384,2048]{1,0:T(8,128)(2,1)}, bf16[384,2048]{1,0:T(8,128)(2,1)S(1)}, u32[]{:S(2)}, u32[]{:S(2)}) collective-permute-start(bf16[384,2048]{1,0:T(8,128)(2,1)} %pad_maximum_fusion.6), channel_id=1, source_target_pairs={{0,1},{1,0},{2,3},{3,2},{4,5},{5,4},{6,7},{7,6},{8,9},{9,8},{10,11... | collective-permute-start | bytes 4718600 | tf_op jit(solution)/shard_map/ppermute | solution.py:22
  273.5 36.7 %collective-permute-start.14 = (bf16[192,2048]{1,0:T(8,128)(2,1)S(1)}, bf16[192,2048]{1,0:T(8,128)(2,1)S(1)}, u32[]{:S(2)}, u32[]{:S(2)}) collective-permute-start(bf16[192,2048]{1,0:T(8,128)(2,1)S(1)} %get-tuple-element.221), channel_id=1, source_target_pairs={{0,2},{1,3},{2,0},{3,1},{4,6},{5,7},{6,4},{7,5},{8,10},{9,11},{10,... | collective-permute-start | bytes 2359304 | tf_op jit(solution)/shard_map/ppermute | solution.py:22
  275.0 35.2 %collective-permute-start.16 = (bf16[192,2048]{1,0:T(8,128)(2,1)S(1)}, bf16[192,2048]{1,0:T(8,128)(2,1)S(1)}, u32[]{:S(2)}, u32[]{:S(2)}) collective-permute-start(bf16[192,2048]{1,0:T(8,128)(2,1)S(1)} %get-tuple-element.222), channel_id=1, source_target_pairs={{0,1},{1,0},{2,3},{3,2},{4,5},{5,4},{6,7},{7,6},{8,9},{9,8},{10,11... | collective-permute-start | bytes 2359304 | tf_op jit(solution)/shard_map/ppermute | solution.py:22
  392.5 312.0 %reduce-scatter.6.cloned.1.call-start = ((), (), s32[]{:S(2)}) async-start(), calls=%async_computation.5 | async-start | bytes 12976128 | tf_op jit(solution)/shard_map/reduce_scatter | solution.py:132
  494.6 33.2 %collective-permute-start.19 = (bf16[384,2048]{1,0:T(8,128)(2,1)S(1)}, bf16[384,2048]{1,0:T(8,128)(2,1)S(1)}, u32[]{:S(2)}, u32[]{:S(2)}) collective-permute-start(bf16[384,2048]{1,0:T(8,128)(2,1)S(1)} %pad_maximum_fusion.7), channel_id=1, source_target_pairs={{0,2},{1,3},{2,0},{3,1},{4,6},{5,7},{6,4},{7,5},{8,10},{9,11},{10,... | collective-permute-start | bytes 4718600 | tf_op jit(solution)/shard_map/ppermute | solution.py:22
  495.3 33.2 %collective-permute-start.20 = (bf16[384,2048]{1,0:T(8,128)(2,1)S(1)}, bf16[384,2048]{1,0:T(8,128)(2,1)}, u32[]{:S(2)}, u32[]{:S(2)}) collective-permute-start(bf16[384,2048]{1,0:T(8,128)(2,1)S(1)} %pad_maximum_fusion.8), channel_id=1, source_target_pairs={{0,1},{1,0},{2,3},{3,2},{4,5},{5,4},{6,7},{7,6},{8,9},{9,8},{10,11... | collective-permute-start | bytes 4718600 | tf_op jit(solution)/shard_map/ppermute | solution.py:22
  528.5 317.8 %reduce-scatter.8.cloned.1.call-start = ((), (), s32[]{:S(2)}) async-start(), calls=%async_computation.6 | async-start | bytes 12976128 | tf_op jit(solution)/shard_map/reduce_scatter | solution.py:132
  588.5 32.9 %collective-permute-start.25 = (bf16[192,2048]{1,0:T(8,128)(2,1)S(1)}, bf16[192,2048]{1,0:T(8,128)(2,1)}, u32[]{:S(2)}, u32[]{:S(2)}) collective-permute-start(bf16[192,2048]{1,0:T(8,128)(2,1)S(1)} %get-tuple-element.263), channel_id=1, source_target_pairs={{0,2},{1,3},{2,0},{3,1},{4,6},{5,7},{6,4},{7,5},{8,10},{9,11},{10,... | collective-permute-start | bytes 2359304 | tf_op jit(solution)/shard_map/ppermute | solution.py:22
  589.5 31.9 %collective-permute-start.26 = (bf16[192,2048]{1,0:T(8,128)(2,1)S(1)}, bf16[192,2048]{1,0:T(8,128)(2,1)}, u32[]{:S(2)}, u32[]{:S(2)}) collective-permute-start(bf16[192,2048]{1,0:T(8,128)(2,1)S(1)} %collective-permute-done.23), channel_id=1, source_target_pairs={{0,2},{1,3},{2,0},{3,1},{4,6},{5,7},{6,4},{7,5},{8,10},{9,11},{10,... | collective-permute-start | bytes 2359304 | tf_op jit(solution)/shard_map/ppermute | solution.py:22
  655.5 49.0 %collective-permute-start.29 = (bf16[384,2048]{1,0:T(8,128)(2,1)}, bf16[384,2048]{1,0:T(8,128)(2,1)}, u32[]{:S(2)}, u32[]{:S(2)}) collective-permute-start(bf16[384,2048]{1,0:T(8,128)(2,1)} %pad_maximum_fusion.9), channel_id=1, source_target_pairs={{0,2},{1,3},{2,0},{3,1},{4,6},{5,7},{6,4},{7,5},{8,10},{9,11},{10,... | collective-permute-start | bytes 4718600 | tf_op jit(solution)/shard_map/ppermute | solution.py:22
  656.4 48.1 %collective-permute-start.30 = (bf16[384,2048]{1,0:T(8,128)(2,1)}, bf16[384,2048]{1,0:T(8,128)(2,1)}, u32[]{:S(2)}, u32[]{:S(2)}) collective-permute-start(bf16[384,2048]{1,0:T(8,128)(2,1)} %pad_maximum_fusion.10), channel_id=1, source_target_pairs={{0,1},{1,0},{2,3},{3,2},{4,5},{5,4},{6,7},{7,6},{8,9},{9,8},{10,11... | collective-permute-start | bytes 4718600 | tf_op jit(solution)/shard_map/ppermute | solution.py:22
  660.6 43.9 %collective-permute-start.31 = (bf16[2,4,4,64,512]{4,3,2,1,0:T(8,128)(2,1)}, bf16[2,4,4,64,512]{4,3,2,1,0:T(8,128)(2,1)}, u32[]{:S(2)}, u32[]{:S(2)}) collective-permute-start(bf16[2,4,4,64,512]{4,3,2,1,0:T(8,128)(2,1)} %dynamic-slice_bitcast_fusion), channel_id=1, source_target_pairs={{0,4},{4,0},{1,5},{5,1},{2,6},{6,2},{3,7},{7,3},{8,12},{12,8},{9,1... | collective-permute-start | bytes 6291464 | tf_op jit(solution)/shard_map/ppermute | solution.py:22
  776.0 69.9 %collective-permute-start.37 = (bf16[1536,512]{1,0:T(8,128)(2,1)}, bf16[1536,512]{1,0:T(8,128)(2,1)}, u32[]{:S(2)}, u32[]{:S(2)}) collective-permute-start(bf16[1536,512]{1,0:T(8,128)(2,1)} %constant_dynamic-update-slice_fusion.5), channel_id=1, source_target_pairs={{0,16},{8,24},{16,0},{24,8},{1,17},{9,25},{17,1},{25,9},{2,18},{10... | collective-permute-start | bytes 4718600 | tf_op jit(solution)/shard_map/ppermute | solution.py:22
  776.8 69.5 %collective-permute-start.38 = (bf16[1536,512]{1,0:T(8,128)(2,1)}, bf16[1536,512]{1,0:T(8,128)(2,1)}, u32[]{:S(2)}, u32[]{:S(2)}) collective-permute-start(bf16[1536,512]{1,0:T(8,128)(2,1)} %pad_maximum_fusion.13), channel_id=1, source_target_pairs={{0,8},{8,0},{16,24},{24,16},{1,9},{9,1},{17,25},{25,17},{2,10},{10... | collective-permute-start | bytes 4718600 | tf_op jit(solution)/shard_map/ppermute | solution.py:22
  780.6 65.7 %collective-permute-start.35 = (bf16[384,2048]{1,0:T(8,128)(2,1)}, bf16[384,2048]{1,0:T(8,128)(2,1)}, u32[]{:S(2)}, u32[]{:S(2)}) collective-permute-start(bf16[384,2048]{1,0:T(8,128)(2,1)} %pad_maximum_fusion.11), channel_id=1, source_target_pairs={{0,2},{1,3},{2,0},{3,1},{4,6},{5,7},{6,4},{7,5},{8,10},{9,11},{10,... | collective-permute-start | bytes 4718600 | tf_op jit(solution)/shard_map/ppermute | solution.py:22
  781.3 65.0 %collective-permute-start.36 = (bf16[384,2048]{1,0:T(8,128)(2,1)}, bf16[384,2048]{1,0:T(8,128)(2,1)}, u32[]{:S(2)}, u32[]{:S(2)}) collective-permute-start(bf16[384,2048]{1,0:T(8,128)(2,1)} %pad_maximum_fusion.12), channel_id=1, source_target_pairs={{0,1},{1,0},{2,3},{3,2},{4,5},{5,4},{6,7},{7,6},{8,9},{9,8},{10,11... | collective-permute-start | bytes 4718600 | tf_op jit(solution)/shard_map/ppermute | solution.py:22
  854.1 32.9 %collective-permute-start.41 = (bf16[768,512]{1,0:T(8,128)(2,1)S(1)}, bf16[768,512]{1,0:T(8,128)(2,1)S(1)}, u32[]{:S(2)}, u32[]{:S(2)}) collective-permute-start(bf16[768,512]{1,0:T(8,128)(2,1)S(1)} %add_convert_fusion.5), channel_id=1, source_target_pairs={{0,8},{8,0},{16,24},{24,16},{1,9},{9,1},{17,25},{25,17},{2,10},{10... | collective-permute-start | bytes 2359304 | tf_op jit(solution)/shard_map/ppermute | solution.py:22
  854.5 35.3 %collective-permute-start.42 = (bf16[768,512]{1,0:T(8,128)(2,1)S(1)}, bf16[768,512]{1,0:T(8,128)(2,1)S(1)}, u32[]{:S(2)}, u32[]{:S(2)}) collective-permute-start(bf16[768,512]{1,0:T(8,128)(2,1)S(1)} %add_convert_fusion.4), channel_id=1, source_target_pairs={{0,16},{8,24},{16,0},{24,8},{1,17},{9,25},{17,1},{25,9},{2,18},{10... | collective-permute-start | bytes 2359304 | tf_op jit(solution)/shard_map/ppermute | solution.py:22
  930.4 44.1 %collective-permute-start.61 = (bf16[512,2048]{1,0:T(8,128)(2,1)S(1)}, bf16[512,2048]{1,0:T(8,128)(2,1)}, u32[]{:S(2)}, u32[]{:S(2)}) collective-permute-start(bf16[512,2048]{1,0:T(8,128)(2,1)S(1)} %maximum_dynamic-update-slice_fusion.20), channel_id=1, source_target_pairs={{0,4},{4,0},{1,5},{5,1},{2,6},{6,2},{3,7},{7,3},{8,12},{12,8},{9,1... | collective-permute-start | bytes 6291464 | tf_op jit(solution)/shard_map/ppermute | solution.py:22
  931.0 43.6 %collective-permute-start.59 = (bf16[144,2048]{1,0:T(8,128)(2,1)S(1)}, bf16[144,2048]{1,0:T(8,128)(2,1)}, u32[]{:S(2)}, u32[]{:S(2)}) collective-permute-start(bf16[144,2048]{1,0:T(8,128)(2,1)S(1)} %get-tuple-element.333), channel_id=1, source_target_pairs={{0,16},{8,24},{16,0},{24,8},{1,17},{9,25},{17,1},{25,9},{2,18},{10... | collective-permute-start | bytes 1769480 | tf_op jit(solution)/shard_map/ppermute | solution.py:22
  935.0 64.9 %collective-permute-start.56 = (bf16[144,2048]{1,0:T(8,128)(2,1)S(1)}, bf16[144,2048]{1,0:T(8,128)(2,1)}, u32[]{:S(2)}, u32[]{:S(2)}) collective-permute-start(bf16[144,2048]{1,0:T(8,128)(2,1)S(1)} %get-tuple-element.332), channel_id=1, source_target_pairs={{0,16},{8,24},{16,0},{24,8},{1,17},{9,25},{17,1},{25,9},{2,18},{10... | collective-permute-start | bytes 1769480 | tf_op jit(solution)/shard_map/ppermute | solution.py:22
  935.1 64.8 %collective-permute-start.58 = (bf16[144,2048]{1,0:T(8,128)(2,1)S(1)}, bf16[144,2048]{1,0:T(8,128)(2,1)}, u32[]{:S(2)}, u32[]{:S(2)}) collective-permute-start(bf16[144,2048]{1,0:T(8,128)(2,1)S(1)} %get-tuple-element.333), channel_id=1, source_target_pairs={{0,8},{8,0},{16,24},{24,16},{1,9},{9,1},{17,25},{25,17},{2,10},{10... | collective-permute-start | bytes 1769480 | tf_op jit(solution)/shard_map/ppermute | solution.py:22
  959.6 52.5 %collective-permute-start.57 = (bf16[144,2048]{1,0:T(8,128)(2,1)}, bf16[144,2048]{1,0:T(8,128)(2,1)}, u32[]{:S(2)}, u32[]{:S(2)}) collective-permute-start(bf16[144,2048]{1,0:T(8,128)(2,1)} %collective-permute-done.55), channel_id=1, source_target_pairs={{0,16},{8,24},{16,0},{24,8},{1,17},{9,25},{17,1},{25,9},{2,18},{10... | collective-permute-start | bytes 1769480 | tf_op jit(solution)/shard_map/ppermute | solution.py:22
  974.6 37.5 %collective-permute-start.60 = (bf16[144,2048]{1,0:T(8,128)(2,1)}, bf16[144,2048]{1,0:T(8,128)(2,1)}, u32[]{:S(2)}, u32[]{:S(2)}) collective-permute-start(bf16[144,2048]{1,0:T(8,128)(2,1)} %collective-permute-done.59), channel_id=1, source_target_pairs={{0,8},{8,0},{16,24},{24,16},{1,9},{9,1},{17,25},{25,17},{2,10},{10... | collective-permute-start | bytes 1769480 | tf_op jit(solution)/shard_map/ppermute | solution.py:22
  (141 other events, 2035.1 us)
Sparse Core Ops, SparseCore 0:
  45.5 65.0 all-gather.5
  119.4 68.7 all-gather.3
  392.6 117.6 reduce-scatter.3
  528.6 117.8 reduce-scatter.5
  648.7 117.6 reduce-scatter.7

commit v2 on v1

--- a/solution.py
+++ b/solution.py
@@ -245,7 +245,6 @@
     queries, (out, stats, bias) = rest[:experts], rest[experts:]
     block, head = pl.program_id(0), pl.program_id(1)
     factor = HEAD ** (-0.5) * LOG2E
-    rows = experts * QUERY_ROWS
 
     def step(at):
         low, high = key_span(at)
@@ -261,18 +260,15 @@
                 low + lax.broadcasted_iota(jnp.int32, shape, 1),
             )
 
-        query = jnp.concatenate([q[0] for q in queries], 0)
-        scores = nt(query, keys[0, low:high])
-        scores = scores + jnp.concatenate([bias[:, :span]] * experts, 0)
-        top = jnp.max(scores, -1, keepdims=True)
-        weights = jnp.exp2((scores - top) * factor)
-        total = jnp.sum(weights, -1, keepdims=True)
-        mixed = nn(weights.astype(BF16), values[0, low:high]) / total
-        level = jnp.broadcast_to(top * factor + jnp.log2(total), (rows, HEAD)).T
         for expert in range(experts):
-            part = slice(expert * QUERY_ROWS, (expert + 1) * QUERY_ROWS)
-            out[expert] = mixed[part].astype(BF16)
-            stats[0, expert : expert + 1, :] = level[0:1, part]
+            scores = nt(queries[expert][0], keys[0, low:high]) + bias[:, :span]
+            top = jnp.max(scores, -1, keepdims=True)
+            weights = jnp.exp2((scores - top) * factor)
+            total = jnp.sum(weights, -1, keepdims=True)
+            mixed = nn(weights.astype(BF16), values[0, low:high]) / total
+            level = jnp.broadcast_to(top * factor + jnp.log2(total), (QUERY_ROWS, HEAD)).T
+            out[expert] = mixed.astype(BF16)
+            stats[0, expert : expert + 1, :] = level[0:1, :]
 
     for at in range(blocks):
         pl.when(block == at)(lambda at=at: step(at))

time: 1060 us -> 1060 us (level)
  transfers between devices with their start and end apart: 68 -> 68, of which waited for: 30 -> 32; matrix products, arithmetic and copies ran while one was open for 38% -> 38% of each run, Pallas kernels for 14% -> 13%
where the time goes in v2:
time: 1060 us; the launch traced here: 1050 us
  matrix products  308 us (29%)
  waiting for transfers between devices  282 us (27%)
  Pallas kernels  162 us (15%)
  other arithmetic  122 us (12%)
  local copies, waits for them, and re-layouts  92.4 us (9%)
  starting transfers between devices  70.9 us (7%)
  between operations  16.3 us (2%)
    dot_general x17, matrix products, mm(): return jnp.einsum(spec, a, b, preferred_element_type=F32)  273 us
    ppermute x63, waiting for transfers between devices, swap(): return lax.ppermute(value, axis, [(i, i ^ bits) for i in range(count)])  269 us
    ppermute x63, starting transfers between devices, swap(): return lax.ppermute(value, axis, [(i, i ^ bits) for i in range(count)])  70.3 us
    pallas_call x1, Pallas kernels, attend_back(): pl.pallas_call(lambda *refs: attend_back_kernel(experts, blocks, *refs),...  42 us
    pallas_call x1, Pallas kernels, attend(): pl.pallas_call(lambda *refs: attend_kernel(experts, blocks, *refs), grid=...  33.3 us
    unnamed x233, local copies, waits for them, and re-layouts  28.5 us
    pallas_call x2, Pallas kernels, swiglu(): pl.pallas_call(lambda *refs: swiglu_kernel(expert, *refs), grid=(seq // r...  25 us
    pallas_call x1, Pallas kernels, heads_back(): pl.pallas_call(heads_back_kernel, grid=(seq // rows,), in_specs=[pl.Block...  22.8 us
  transfers between devices with their start and end apart: 68, of which 32 were waited for; matrix products, arithmetic and copies ran while one was open for 38% of the time, Pallas kernels for 13%

profile of v2, /device:TPU:0, one launch (start us, length us, event | category | flops | bytes accessed | tf_op | source)
XLA Modules:
  0.0 1053.8 jit_solution(16750802410453166787)
XLA Ops:
  24.4 13.1 %slice_bitcast_fusion = (bf16[2048,1408]{1,0:T(8,128)(2,1)}, bf16[2048,1408]{1,0:T(8,128)(2,1)S(1)}, bf16[2048,1408]{1,0:T(8,128)(2,1)S(1)}, bf16[2048,1408]{1,0:T(8,128)(2,1)}) fusion(bf16[2,2048,1408]{2,1,0:T(8,128)(2,1)} %param.23, bf16[2,2048,1408]{2,1,0:T(8,128)(2,1)} %param.22), kind=kLoop, calls=%fused_computation.24 | loop fusion | bytes 46137344 | tf_op jit(solution)/shard_map/unstack | solution.py:716
  71.8 14.5 %collective-permute-done.6 = bf16[192,2048]{1,0:T(8,128)(2,1)} collective-permute-done((bf16[192,2048]{1,0:T(8,128)(2,1)}, bf16[192,2048]{1,0:T(8,128)(2,1)}, u32[]{:S(2)}, u32[]{:S(2)}) %collective-permute-start.6) | collective-permute-done | bytes 786464 | tf_op jit(solution)/shard_map/ppermute | solution.py:22
  128.4 21.3 %shard_map.220.refs_2_.refs_3_.refs_4_.refs_5_.refs_6_.refs_7_ = bf16[4,1536,512]{2,1,0:T(8,128)(2,1)} custom-call(bf16[1536,2048]{1,0:T(8,128)(2,1)} %fusion.2.normed, bf16[4,2048,512]{2,1,0:T(8,128)(2,1)} %constant_dynamic-update-slice_fusion.weight, f32[1536,128]{1,0:T(8,128)S(1)} %get-tuple-element.200.cos.refs_2_, ...), custom_call_target="tpu_custom_call" | custom-call | flops 12884901888 | bytes 20971520 | tf_op jit(solution)/shard_map/pallas_call | solution.py:213
  149.7 33.3 %shard_map.221 = (bf16[2,1536,512]{2,1,0:T(8,128)(2,1)S(1)}, f32[4,2,1536]{2,1,0:T(2,128)S(1)}) custom-call(s32[1536,1]{1,0:T(8,128)S(1)} %bitcast.325, s32[1,1536]{1,0:T(1,128)S(1)} %bitcast.328, bf16[4,1536,512]{2,1,0:T(8,128)(2,1)} %shard_map.220.refs_2_.refs_3_.refs_4_.refs_5_.refs_6_.refs_7_, ...), custom_call_target="tpu_custom_call" | custom-call | flops 10737418240 | bytes 9437184 | tf_op jit(solution)/shard_map/pallas_call | solution.py:285
  211.0 15.6 %convolution_convert_fusion.9.refs_2_ = bf16[1536,1408]{1,0:T(8,128)(2,1)} fusion(bf16[1536,2048]{1,0:T(8,128)(2,1)} %all-gather.4.cloned.1.call-done, bf16[2,1408,2048]{2,1,0:T(8,128)(2,1)} %param.24), kind=kOutput, calls=%fused_computation.20 | convolution fusion | flops 8860532736 | bytes 16384000 | tf_op jit(solution)/shard_map/td,fd->tf/dot_general | solution.py:607
  226.6 18.7 %collective-permute-done.9 = bf16[384,2048]{1,0:T(8,128)(2,1)S(1)} collective-permute-done((bf16[384,2048]{1,0:T(8,128)(2,1)}, bf16[384,2048]{1,0:T(8,128)(2,1)S(1)}, u32[]{:S(2)}, u32[]{:S(2)}) %collective-permute-start.9) | collective-permute-done | bytes 1572896 | tf_op jit(solution)/shard_map/ppermute | solution.py:22
  254.5 10.7 %collective-permute-done.11 = bf16[192,2048]{1,0:T(8,128)(2,1)S(1)} collective-permute-done((bf16[192,2048]{1,0:T(8,128)(2,1)S(1)}, bf16[192,2048]{1,0:T(8,128)(2,1)S(1)}, u32[]{:S(2)}, u32[]{:S(2)}) %collective-permute-start.11) | collective-permute-done | bytes 786464 | tf_op jit(solution)/shard_map/ppermute | solution.py:22
  273.8 16.3 %collective-permute-done.13 = bf16[192,2048]{1,0:T(8,128)(2,1)S(1)} collective-permute-done((bf16[192,2048]{1,0:T(8,128)(2,1)S(1)}, bf16[192,2048]{1,0:T(8,128)(2,1)S(1)}, u32[]{:S(2)}, u32[]{:S(2)}) %collective-permute-start.13) | collective-permute-done | bytes 786464 | tf_op jit(solution)/shard_map/ppermute | solution.py:22
  292.1 15.1 %convolution_convert_fusion.8.refs_2_ = bf16[1536,1408]{1,0:T(8,128)(2,1)} fusion(bf16[1536,2048]{1,0:T(8,128)(2,1)} %all-gather.4.cloned.1.call-done, bf16[2,1408,2048]{2,1,0:T(8,128)(2,1)} %param.24), kind=kOutput, calls=%fused_computation.19 | convolution fusion | flops 8860532736 | bytes 16384000 | tf_op jit(solution)/shard_map/td,fd->tf/dot_general | solution.py:607
  308.4 13.1 %collective-permute-done.15 = bf16[192,2048]{1,0:T(8,128)(2,1)} collective-permute-done((bf16[192,2048]{1,0:T(8,128)(2,1)S(1)}, bf16[192,2048]{1,0:T(8,128)(2,1)}, u32[]{:S(2)}, u32[]{:S(2)}) %collective-permute-start.15) | collective-permute-done | bytes 786464 | tf_op jit(solution)/shard_map/ppermute | solution.py:22
  323.8 11.4 %convolution_convert_fusion.6.refs_1_ = bf16[1536,1408]{1,0:T(8,128)(2,1)} fusion(bf16[1536,2048]{1,0:T(8,128)(2,1)S(1)} %maximum_dynamic-update-slice_fusion.8, bf16[2,2048,1408]{2,1,0:T(8,128)(2,1)S(1)} %bitcast.344), kind=kOutput, calls=%fused_computation.17 | convolution fusion | flops 8860532736 | bytes 16384000 | tf_op jit(solution)/shard_map/td,df->tf/dot_general | solution.py:607
  335.2 13.7 %convolution_convert_fusion.7.refs_0_ = bf16[1536,1408]{1,0:T(8,128)(2,1)} fusion(bf16[1536,2048]{1,0:T(8,128)(2,1)S(1)} %maximum_dynamic-update-slice_fusion.8, bf16[2,2048,1408]{2,1,0:T(8,128)(2,1)} %param.22), kind=kOutput, calls=%fused_computation.18 | convolution fusion | flops 8860532736 | bytes 16384000 | tf_op jit(solution)/shard_map/td,df->tf/dot_general | solution.py:607
  352.0 12.6 %shard_map.222 = (bf16[1536,2816]{1,0:T(8,128)(2,1)}, bf16[1536,1408]{1,0:T(8,128)(2,1)S(1)}, f32[1536,1]{1,0:T(8,128)S(1)}) custom-call(bf16[1536,1408]{1,0:T(8,128)(2,1)} %convolution_convert_fusion.7.refs_0_, bf16[1536,1408]{1,0:T(8,128)(2,1)} %convolution_convert_fusion.6.refs_1_, bf16[1536,1408]{1,0:T(8,128)(2,1)} %convolution_convert_fusion.9.refs_2_, ...), custom_call_target="tpu_custom_call" | custom-call | flops 43253760 | bytes 25952256 | tf_op jit(solution)/shard_map/pallas_call | solution.py:453
  364.6 25.5 %convolution_convert_fusion.2 = bf16[2816,2048]{1,0:T(8,128)(2,1)} fusion(bf16[1536,2816]{1,0:T(8,128)(2,1)} %get-tuple-element.230, bf16[1536,2048]{1,0:T(8,128)(2,1)S(1)} %bitcast.333), kind=kOutput, calls=%fused_computation.13 | convolution fusion | flops 17722507264 | bytes 26476544 | tf_op jit(solution)/shard_map/tf,td->fd/dot_general | solution.py:607
  390.5 15.4 %convolution_convert_fusion.4.refs_1_ = bf16[1536,1408]{1,0:T(8,128)(2,1)} fusion(bf16[1536,2048]{1,0:T(8,128)(2,1)} %copy-done.14, bf16[2,2048,1408]{2,1,0:T(8,128)(2,1)} %param.23), kind=kOutput, calls=%fused_computation.15 | convolution fusion | flops 8860532736 | bytes 16384000 | tf_op jit(solution)/shard_map/td,df->tf/dot_general | solution.py:607
  406.0 15.1 %convolution_convert_fusion.5.refs_0_ = bf16[1536,1408]{1,0:T(8,128)(2,1)} fusion(bf16[1536,2048]{1,0:T(8,128)(2,1)} %copy-done.14, bf16[2,2048,1408]{2,1,0:T(8,128)(2,1)} %param.22), kind=kOutput, calls=%fused_computation.16 | convolution fusion | flops 8860532736 | bytes 16384000 | tf_op jit(solution)/shard_map/td,df->tf/dot_general | solution.py:607
  421.0 12.3 %shard_map.223 = (bf16[1536,2816]{1,0:T(8,128)(2,1)}, bf16[1536,1408]{1,0:T(8,128)(2,1)S(1)}, f32[1536,1]{1,0:T(8,128)S(1)}) custom-call(bf16[1536,1408]{1,0:T(8,128)(2,1)} %convolution_convert_fusion.5.refs_0_, bf16[1536,1408]{1,0:T(8,128)(2,1)} %convolution_convert_fusion.4.refs_1_, bf16[1536,1408]{1,0:T(8,128)(2,1)} %convolution_convert_fusion.8.refs_2_, ...), custom_call_target="tpu_custom_call" | custom-call | flops 43253760 | bytes 25952256 | tf_op jit(solution)/shard_map/pallas_call | solution.py:453
  438.2 25.0 %fusion.73 = f32[1536,2048]{1,0:T(8,128)} fusion(bf16[1536,2816]{1,0:T(8,128)(2,1)} %get-tuple-element.241, bf16[2048,2816]{1,0:T(8,128)(2,1)} %pad_maximum_fusion.1), kind=kOutput, calls=%fused_computation.313 | convolution fusion | flops 17716740096 | bytes 32768000 | tf_op jit(solution)/shard_map/tf,df->td/dot_general | solution.py:607
  463.2 26.6 %add_convert_fusion = bf16[1536,2048]{1,0:T(8,128)(2,1)} fusion(f32[1536,2048]{1,0:T(8,128)} %fusion.73, bf16[1536,2816]{1,0:T(8,128)(2,1)} %get-tuple-element.230, bf16[2048,2816]{1,0:T(8,128)(2,1)} %pad_maximum_fusion, f32[2048]{0:T(1024)S(1)} %bitcast.423, f32[1536]{0:T(1024)S(1)} %get-tuple-element.353, f32[2048]{0:T(1024)S(1)} %bitcast.422, ...), kind=kOutput, calls=%fused_computation.7 | convolution fusion | flops 17735614464 | bytes 39088128 | tf_op jit(solution)/shard_map/tf,df->td/dot_general | solution.py:607
  494.5 24.6 %convolution_convert_fusion.1 = bf16[2816,2048]{1,0:T(8,128)(2,1)} fusion(bf16[1536,2816]{1,0:T(8,128)(2,1)} %get-tuple-element.241, bf16[1536,2048]{1,0:T(8,128)(2,1)} %copy-done.14), kind=kOutput, calls=%fused_computation.12 | convolution fusion | flops 17722507264 | bytes 26476544 | tf_op jit(solution)/shard_map/tf,td->fd/dot_general | solution.py:607
  562.9 21.1 %convolution_convert_fusion = bf16[2816,2048]{1,0:T(8,128)(2,1)} fusion(bf16[1536,2816]{1,0:T(8,128)(2,1)S(1)} %constant_dynamic-update-slice_fusion.3, bf16[1536,2048]{1,0:T(8,128)(2,1)S(1)} %bitcast.430), kind=kOutput, calls=%fused_computation.11 | convolution fusion | flops 17722507264 | bytes 26476544 | tf_op jit(solution)/shard_map/tf,td->fd/dot_general | solution.py:607
  588.9 23.6 %convolution_convert_fusion.3 = bf16[1536,2048]{1,0:T(8,128)(2,1)S(1)} fusion(bf16[1536,2816]{1,0:T(8,128)(2,1)} %copy-done.34, bf16[2816,2048]{1,0:T(8,128)(2,1)} %bitcast.428), kind=kOutput, calls=%fused_computation.14 | convolution fusion | flops 17719885824 | bytes 26476544 | tf_op jit(solution)/shard_map/tf,fd->td/dot_general | solution.py:607
  626.8 22.8 %shard_map.224 = (bf16[2,1536,512]{2,1,0:T(8,128)(2,1)}, f32[16,1536]{1,0:T(8,128)}, bf16[2,2,4,4,64,512]{5,4,3,2,1,0:T(8,128)(2,1)}) custom-call(bf16[1536,2048]{1,0:T(8,128)(2,1)} %maximum_dynamic-update-slice_fusion.12.d_middle, bf16[2,512,2048]{2,1,0:T(8,128)(2,1)} %out_weight.1, bf16[2,1536,512]{2,1,0:T(8,128)(2,1)} %copy-done.10, f32[1536,2]{1,0:T(8,128)} %copy-done.27), custom_call_target="tpu_custom_call" | custom-call | flops 12884901888 | bytes 20971520 | tf_op jit(solution)/shard_map/pallas_call | solution.py:522
  659.0 42.0 %shard_map.225 = bf16[4,1536,512]{2,1,0:T(8,128)(2,1)} custom-call(s32[1,1536]{1,0:T(1,128)S(1)} %bitcast.329, s32[1536,1]{1,0:T(8,128)S(1)} %bitcast.326, f32[1536,128]{1,0:T(8,128)S(1)} %copy-done.7, f32[1536,128]{1,0:T(8,128)S(1)} %get-tuple-element.201.sin.refs_3_, bf16[4,1536,512]{2,1,0:T(8,128)(2,1)} %shard_map.220.refs_2_.refs_3_.refs_4_.refs_5_.refs_6_.refs_7_, ...), custom_call_target="tpu_custom_call" | custom-call | flops 26843545600 | bytes 15728640 | tf_op jit(solution)/shard_map/pallas_call | solution.py:371
  733.5 18.8 %fusion.3 = bf16[1536,2048]{1,0:T(8,128)(2,1)S(1)} fusion(bf16[4,1536,512]{2,1,0:T(8,128)(2,1)} %shard_map.225, bf16[4,2048,512]{2,1,0:T(8,128)(2,1)} %constant_dynamic-update-slice_fusion.weight, f32[2048]{0:T(1024)S(1)} %bitcast.421, f32[1536]{0:T(1024)S(1)} %get-tuple-element.351, f32[2048]{0:T(1024)S(1)} %bitcast.420, f32[1536]{0:T(1024)S(1)} %get-tuple-element.350), kind=kOutput, calls=%fused_computation.6 | convolution fusion | flops 12900630528 | bytes 21000192 | tf_op jit(solution)/shard_map/ktf,kdf->td/dot_general | solution.py:607
  786.6 56.3 %collective-permute-done.37 = bf16[1536,512]{1,0:T(8,128)(2,1)} collective-permute-done((bf16[1536,512]{1,0:T(8,128)(2,1)}, bf16[1536,512]{1,0:T(8,128)(2,1)}, u32[]{:S(2)}, u32[]{:S(2)}) %collective-permute-start.37) | collective-permute-done | bytes 1572896 | tf_op jit(solution)/shard_map/ppermute | solution.py:22
  868.0 16.9 %collective-permute-done.41 = bf16[768,512]{1,0:T(8,128)(2,1)S(1)} collective-permute-done((bf16[768,512]{1,0:T(8,128)(2,1)S(1)}, bf16[768,512]{1,0:T(8,128)(2,1)S(1)}, u32[]{:S(2)}, u32[]{:S(2)}) %collective-permute-start.41) | collective-permute-done | bytes 786464 | tf_op jit(solution)/shard_map/ppermute | solution.py:22
  936.5 23.6 %collective-permute-done.55 = bf16[144,2048]{1,0:T(8,128)(2,1)} collective-permute-done((bf16[144,2048]{1,0:T(8,128)(2,1)S(1)}, bf16[144,2048]{1,0:T(8,128)(2,1)}, u32[]{:S(2)}, u32[]{:S(2)}) %collective-permute-start.55) | collective-permute-done | bytes 589856 | tf_op jit(solution)/shard_map/ppermute | solution.py:22
  960.1 15.8 %collective-permute-done.59 = bf16[144,2048]{1,0:T(8,128)(2,1)} collective-permute-done((bf16[144,2048]{1,0:T(8,128)(2,1)S(1)}, bf16[144,2048]{1,0:T(8,128)(2,1)}, u32[]{:S(2)}, u32[]{:S(2)}) %collective-permute-start.59) | collective-permute-done | bytes 589856 | tf_op jit(solution)/shard_map/ppermute | solution.py:22
  983.0 18.2 %collective-permute-done.56 = bf16[144,2048]{1,0:T(8,128)(2,1)} collective-permute-done((bf16[144,2048]{1,0:T(8,128)(2,1)S(1)}, bf16[144,2048]{1,0:T(8,128)(2,1)}, u32[]{:S(2)}, u32[]{:S(2)}) %collective-permute-start.56) | collective-permute-done | bytes 589856 | tf_op jit(solution)/shard_map/ppermute | solution.py:22
  1001.2 12.2 %collective-permute-done.57 = bf16[144,2048]{1,0:T(8,128)(2,1)} collective-permute-done((bf16[144,2048]{1,0:T(8,128)(2,1)}, bf16[144,2048]{1,0:T(8,128)(2,1)}, u32[]{:S(2)}, u32[]{:S(2)}) %collective-permute-start.57) | collective-permute-done | bytes 589856 | tf_op jit(solution)/shard_map/ppermute | solution.py:22
  1035.5 10.4 shard_map.227
  (560 shorter events, 401.9 us)
Async XLA Ops:
  7.2 103.3 %all-gather.6.cloned.1.call-start = ((), (), s32[]{:S(2)}) async-start(), calls=%async_computation.7 | async-start | bytes 7077888 | tf_op jit(solution)/shard_map/all_gather | solution.py:673
  9.7 33.9 %collective-permute-start.3 = (bf16[192,2048]{1,0:T(8,128)(2,1)}, bf16[192,2048]{1,0:T(8,128)(2,1)}, u32[]{:S(2)}, u32[]{:S(2)}) collective-permute-start(bf16[192,2048]{1,0:T(8,128)(2,1)} %get-tuple-element.185), channel_id=1, source_target_pairs={{0,1},{1,0},{2,3},{3,2},{4,5},{5,4},{6,7},{7,6},{8,9},{9,8},{10,11... | collective-permute-start | bytes 2359304 | tf_op jit(solution)/shard_map/ppermute | solution.py:22
  45.3 142.9 %all-gather.4.cloned.1.call-start = ((), (), s32[]{:S(2)}) async-start(), calls=%async_computation.3 | async-start | bytes 7864320 | tf_op jit(solution)/shard_map/all_gather | solution.py:705
  52.5 33.7 %collective-permute-start.6 = (bf16[192,2048]{1,0:T(8,128)(2,1)}, bf16[192,2048]{1,0:T(8,128)(2,1)}, u32[]{:S(2)}, u32[]{:S(2)}) collective-permute-start(bf16[192,2048]{1,0:T(8,128)(2,1)} %collective-permute-done.3), channel_id=1, source_target_pairs={{0,2},{1,3},{2,0},{3,1},{4,6},{5,7},{6,4},{7,5},{8,10},{9,11},{10,... | collective-permute-start | bytes 2359304 | tf_op jit(solution)/shard_map/ppermute | solution.py:22
  53.0 33.2 %collective-permute-start.7 = (bf16[192,2048]{1,0:T(8,128)(2,1)S(1)}, bf16[192,2048]{1,0:T(8,128)(2,1)}, u32[]{:S(2)}, u32[]{:S(2)}) collective-permute-start(bf16[192,2048]{1,0:T(8,128)(2,1)S(1)} %get-tuple-element.186), channel_id=1, source_target_pairs={{0,1},{1,0},{2,3},{3,2},{4,5},{5,4},{6,7},{7,6},{8,9},{9,8},{10,11... | collective-permute-start | bytes 2359304 | tf_op jit(solution)/shard_map/ppermute | solution.py:22
  53.5 34.0 %collective-permute-start.8 = (bf16[192,2048]{1,0:T(8,128)(2,1)}, bf16[192,2048]{1,0:T(8,128)(2,1)}, u32[]{:S(2)}, u32[]{:S(2)}) collective-permute-start(bf16[192,2048]{1,0:T(8,128)(2,1)} %collective-permute-done.4), channel_id=1, source_target_pairs={{0,1},{1,0},{2,3},{3,2},{4,5},{5,4},{6,7},{7,6},{8,9},{9,8},{10,11... | collective-permute-start | bytes 2359304 | tf_op jit(solution)/shard_map/ppermute | solution.py:22
  119.3 428.5 %reduce-scatter.4.cloned.1.call-start = ((), (), s32[]{:S(2)}) async-start(), calls=%async_computation.4 | async-start | bytes 12976128 | tf_op jit(solution)/shard_map/reduce_scatter | solution.py:132
  208.9 36.3 %collective-permute-start.9 = (bf16[384,2048]{1,0:T(8,128)(2,1)}, bf16[384,2048]{1,0:T(8,128)(2,1)S(1)}, u32[]{:S(2)}, u32[]{:S(2)}) collective-permute-start(bf16[384,2048]{1,0:T(8,128)(2,1)} %pad_maximum_fusion.5), channel_id=1, source_target_pairs={{0,2},{1,3},{2,0},{3,1},{4,6},{5,7},{6,4},{7,5},{8,10},{9,11},{10,... | collective-permute-start | bytes 4718600 | tf_op jit(solution)/shard_map/ppermute | solution.py:22
  210.4 36.1 %collective-permute-start.10 = (bf16[384,2048]{1,0:T(8,128)(2,1)}, bf16[384,2048]{1,0:T(8,128)(2,1)S(1)}, u32[]{:S(2)}, u32[]{:S(2)}) collective-permute-start(bf16[384,2048]{1,0:T(8,128)(2,1)} %pad_maximum_fusion.6), channel_id=1, source_target_pairs={{0,1},{1,0},{2,3},{3,2},{4,5},{5,4},{6,7},{7,6},{8,9},{9,8},{10,11... | collective-permute-start | bytes 4718600 | tf_op jit(solution)/shard_map/ppermute | solution.py:22
  271.7 36.7 %collective-permute-start.14 = (bf16[192,2048]{1,0:T(8,128)(2,1)S(1)}, bf16[192,2048]{1,0:T(8,128)(2,1)S(1)}, u32[]{:S(2)}, u32[]{:S(2)}) collective-permute-start(bf16[192,2048]{1,0:T(8,128)(2,1)S(1)} %get-tuple-element.221), channel_id=1, source_target_pairs={{0,2},{1,3},{2,0},{3,1},{4,6},{5,7},{6,4},{7,5},{8,10},{9,11},{10,... | collective-permute-start | bytes 2359304 | tf_op jit(solution)/shard_map/ppermute | solution.py:22
  273.2 35.2 %collective-permute-start.16 = (bf16[192,2048]{1,0:T(8,128)(2,1)S(1)}, bf16[192,2048]{1,0:T(8,128)(2,1)S(1)}, u32[]{:S(2)}, u32[]{:S(2)}) collective-permute-start(bf16[192,2048]{1,0:T(8,128)(2,1)S(1)} %get-tuple-element.222), channel_id=1, source_target_pairs={{0,1},{1,0},{2,3},{3,2},{4,5},{5,4},{6,7},{7,6},{8,9},{9,8},{10,11... | collective-permute-start | bytes 2359304 | tf_op jit(solution)/shard_map/ppermute | solution.py:22
  390.2 310.8 %reduce-scatter.6.cloned.1.call-start = ((), (), s32[]{:S(2)}) async-start(), calls=%async_computation.5 | async-start | bytes 12976128 | tf_op jit(solution)/shard_map/reduce_scatter | solution.py:132
  492.2 32.6 %collective-permute-start.19 = (bf16[384,2048]{1,0:T(8,128)(2,1)S(1)}, bf16[384,2048]{1,0:T(8,128)(2,1)S(1)}, u32[]{:S(2)}, u32[]{:S(2)}) collective-permute-start(bf16[384,2048]{1,0:T(8,128)(2,1)S(1)} %pad_maximum_fusion.7), channel_id=1, source_target_pairs={{0,2},{1,3},{2,0},{3,1},{4,6},{5,7},{6,4},{7,5},{8,10},{9,11},{10,... | collective-permute-start | bytes 4718600 | tf_op jit(solution)/shard_map/ppermute | solution.py:22
  493.1 32.4 %collective-permute-start.20 = (bf16[384,2048]{1,0:T(8,128)(2,1)S(1)}, bf16[384,2048]{1,0:T(8,128)(2,1)}, u32[]{:S(2)}, u32[]{:S(2)}) collective-permute-start(bf16[384,2048]{1,0:T(8,128)(2,1)S(1)} %pad_maximum_fusion.8), channel_id=1, source_target_pairs={{0,1},{1,0},{2,3},{3,2},{4,5},{5,4},{6,7},{7,6},{8,9},{9,8},{10,11... | collective-permute-start | bytes 4718600 | tf_op jit(solution)/shard_map/ppermute | solution.py:22
  525.4 317.6 %reduce-scatter.8.cloned.1.call-start = ((), (), s32[]{:S(2)}) async-start(), calls=%async_computation.6 | async-start | bytes 12976128 | tf_op jit(solution)/shard_map/reduce_scatter | solution.py:132
  584.9 32.9 %collective-permute-start.25 = (bf16[192,2048]{1,0:T(8,128)(2,1)S(1)}, bf16[192,2048]{1,0:T(8,128)(2,1)}, u32[]{:S(2)}, u32[]{:S(2)}) collective-permute-start(bf16[192,2048]{1,0:T(8,128)(2,1)S(1)} %get-tuple-element.263), channel_id=1, source_target_pairs={{0,2},{1,3},{2,0},{3,1},{4,6},{5,7},{6,4},{7,5},{8,10},{9,11},{10,... | collective-permute-start | bytes 2359304 | tf_op jit(solution)/shard_map/ppermute | solution.py:22
  585.7 32.0 %collective-permute-start.26 = (bf16[192,2048]{1,0:T(8,128)(2,1)S(1)}, bf16[192,2048]{1,0:T(8,128)(2,1)}, u32[]{:S(2)}, u32[]{:S(2)}) collective-permute-start(bf16[192,2048]{1,0:T(8,128)(2,1)S(1)} %collective-permute-done.23), channel_id=1, source_target_pairs={{0,2},{1,3},{2,0},{3,1},{4,6},{5,7},{6,4},{7,5},{8,10},{9,11},{10,... | collective-permute-start | bytes 2359304 | tf_op jit(solution)/shard_map/ppermute | solution.py:22
  651.8 49.2 %collective-permute-start.29 = (bf16[384,2048]{1,0:T(8,128)(2,1)}, bf16[384,2048]{1,0:T(8,128)(2,1)}, u32[]{:S(2)}, u32[]{:S(2)}) collective-permute-start(bf16[384,2048]{1,0:T(8,128)(2,1)} %pad_maximum_fusion.9), channel_id=1, source_target_pairs={{0,2},{1,3},{2,0},{3,1},{4,6},{5,7},{6,4},{7,5},{8,10},{9,11},{10,... | collective-permute-start | bytes 4718600 | tf_op jit(solution)/shard_map/ppermute | solution.py:22
  652.7 48.4 %collective-permute-start.30 = (bf16[384,2048]{1,0:T(8,128)(2,1)}, bf16[384,2048]{1,0:T(8,128)(2,1)}, u32[]{:S(2)}, u32[]{:S(2)}) collective-permute-start(bf16[384,2048]{1,0:T(8,128)(2,1)} %pad_maximum_fusion.10), channel_id=1, source_target_pairs={{0,1},{1,0},{2,3},{3,2},{4,5},{5,4},{6,7},{7,6},{8,9},{9,8},{10,11... | collective-permute-start | bytes 4718600 | tf_op jit(solution)/shard_map/ppermute | solution.py:22
  657.1 43.9 %collective-permute-start.31 = (bf16[2,4,4,64,512]{4,3,2,1,0:T(8,128)(2,1)}, bf16[2,4,4,64,512]{4,3,2,1,0:T(8,128)(2,1)}, u32[]{:S(2)}, u32[]{:S(2)}) collective-permute-start(bf16[2,4,4,64,512]{4,3,2,1,0:T(8,128)(2,1)} %dynamic-slice_bitcast_fusion), channel_id=1, source_target_pairs={{0,4},{4,0},{1,5},{5,1},{2,6},{6,2},{3,7},{7,3},{8,12},{12,8},{9,1... | collective-permute-start | bytes 6291464 | tf_op jit(solution)/shard_map/ppermute | solution.py:22
  772.3 70.7 %collective-permute-start.37 = (bf16[1536,512]{1,0:T(8,128)(2,1)}, bf16[1536,512]{1,0:T(8,128)(2,1)}, u32[]{:S(2)}, u32[]{:S(2)}) collective-permute-start(bf16[1536,512]{1,0:T(8,128)(2,1)} %constant_dynamic-update-slice_fusion.5), channel_id=1, source_target_pairs={{0,16},{8,24},{16,0},{24,8},{1,17},{9,25},{17,1},{25,9},{2,18},{10... | collective-permute-start | bytes 4718600 | tf_op jit(solution)/shard_map/ppermute | solution.py:22
  774.7 68.4 %collective-permute-start.38 = (bf16[1536,512]{1,0:T(8,128)(2,1)}, bf16[1536,512]{1,0:T(8,128)(2,1)}, u32[]{:S(2)}, u32[]{:S(2)}) collective-permute-start(bf16[1536,512]{1,0:T(8,128)(2,1)} %pad_maximum_fusion.13), channel_id=1, source_target_pairs={{0,8},{8,0},{16,24},{24,16},{1,9},{9,1},{17,25},{25,17},{2,10},{10... | collective-permute-start | bytes 4718600 | tf_op jit(solution)/shard_map/ppermute | solution.py:22
  779.0 64.1 %collective-permute-start.35 = (bf16[384,2048]{1,0:T(8,128)(2,1)}, bf16[384,2048]{1,0:T(8,128)(2,1)}, u32[]{:S(2)}, u32[]{:S(2)}) collective-permute-start(bf16[384,2048]{1,0:T(8,128)(2,1)} %pad_maximum_fusion.11), channel_id=1, source_target_pairs={{0,2},{1,3},{2,0},{3,1},{4,6},{5,7},{6,4},{7,5},{8,10},{9,11},{10,... | collective-permute-start | bytes 4718600 | tf_op jit(solution)/shard_map/ppermute | solution.py:22
  779.8 63.2 %collective-permute-start.36 = (bf16[384,2048]{1,0:T(8,128)(2,1)}, bf16[384,2048]{1,0:T(8,128)(2,1)}, u32[]{:S(2)}, u32[]{:S(2)}) collective-permute-start(bf16[384,2048]{1,0:T(8,128)(2,1)} %pad_maximum_fusion.12), channel_id=1, source_target_pairs={{0,1},{1,0},{2,3},{3,2},{4,5},{5,4},{6,7},{7,6},{8,9},{9,8},{10,11... | collective-permute-start | bytes 4718600 | tf_op jit(solution)/shard_map/ppermute | solution.py:22
  850.6 34.4 %collective-permute-start.41 = (bf16[768,512]{1,0:T(8,128)(2,1)S(1)}, bf16[768,512]{1,0:T(8,128)(2,1)S(1)}, u32[]{:S(2)}, u32[]{:S(2)}) collective-permute-start(bf16[768,512]{1,0:T(8,128)(2,1)S(1)} %add_convert_fusion.5), channel_id=1, source_target_pairs={{0,8},{8,0},{16,24},{24,16},{1,9},{9,1},{17,25},{25,17},{2,10},{10... | collective-permute-start | bytes 2359304 | tf_op jit(solution)/shard_map/ppermute | solution.py:22
  852.0 36.1 %collective-permute-start.42 = (bf16[768,512]{1,0:T(8,128)(2,1)S(1)}, bf16[768,512]{1,0:T(8,128)(2,1)S(1)}, u32[]{:S(2)}, u32[]{:S(2)}) collective-permute-start(bf16[768,512]{1,0:T(8,128)(2,1)S(1)} %add_convert_fusion.4), channel_id=1, source_target_pairs={{0,16},{8,24},{16,0},{24,8},{1,17},{9,25},{17,1},{25,9},{2,18},{10... | collective-permute-start | bytes 2359304 | tf_op jit(solution)/shard_map/ppermute | solution.py:22
  930.9 45.0 %collective-permute-start.61 = (bf16[512,2048]{1,0:T(8,128)(2,1)S(1)}, bf16[512,2048]{1,0:T(8,128)(2,1)}, u32[]{:S(2)}, u32[]{:S(2)}) collective-permute-start(bf16[512,2048]{1,0:T(8,128)(2,1)S(1)} %maximum_dynamic-update-slice_fusion.20), channel_id=1, source_target_pairs={{0,4},{4,0},{1,5},{5,1},{2,6},{6,2},{3,7},{7,3},{8,12},{12,8},{9,1... | collective-permute-start | bytes 6291464 | tf_op jit(solution)/shard_map/ppermute | solution.py:22
  931.5 44.4 %collective-permute-start.59 = (bf16[144,2048]{1,0:T(8,128)(2,1)S(1)}, bf16[144,2048]{1,0:T(8,128)(2,1)}, u32[]{:S(2)}, u32[]{:S(2)}) collective-permute-start(bf16[144,2048]{1,0:T(8,128)(2,1)S(1)} %get-tuple-element.333), channel_id=1, source_target_pairs={{0,16},{8,24},{16,0},{24,8},{1,17},{9,25},{17,1},{25,9},{2,18},{10... | collective-permute-start | bytes 1769480 | tf_op jit(solution)/shard_map/ppermute | solution.py:22
  936.3 64.9 %collective-permute-start.56 = (bf16[144,2048]{1,0:T(8,128)(2,1)S(1)}, bf16[144,2048]{1,0:T(8,128)(2,1)}, u32[]{:S(2)}, u32[]{:S(2)}) collective-permute-start(bf16[144,2048]{1,0:T(8,128)(2,1)S(1)} %get-tuple-element.332), channel_id=1, source_target_pairs={{0,16},{8,24},{16,0},{24,8},{1,17},{9,25},{17,1},{25,9},{2,18},{10... | collective-permute-start | bytes 1769480 | tf_op jit(solution)/shard_map/ppermute | solution.py:22
  936.4 64.8 %collective-permute-start.58 = (bf16[144,2048]{1,0:T(8,128)(2,1)S(1)}, bf16[144,2048]{1,0:T(8,128)(2,1)}, u32[]{:S(2)}, u32[]{:S(2)}) collective-permute-start(bf16[144,2048]{1,0:T(8,128)(2,1)S(1)} %get-tuple-element.333), channel_id=1, source_target_pairs={{0,8},{8,0},{16,24},{24,16},{1,9},{9,1},{17,25},{25,17},{2,10},{10... | collective-permute-start | bytes 1769480 | tf_op jit(solution)/shard_map/ppermute | solution.py:22
  960.1 53.3 %collective-permute-start.57 = (bf16[144,2048]{1,0:T(8,128)(2,1)}, bf16[144,2048]{1,0:T(8,128)(2,1)}, u32[]{:S(2)}, u32[]{:S(2)}) collective-permute-start(bf16[144,2048]{1,0:T(8,128)(2,1)} %collective-permute-done.55), channel_id=1, source_target_pairs={{0,16},{8,24},{16,0},{24,8},{1,17},{9,25},{17,1},{25,9},{2,18},{10... | collective-permute-start | bytes 1769480 | tf_op jit(solution)/shard_map/ppermute | solution.py:22
  975.9 37.5 %collective-permute-start.60 = (bf16[144,2048]{1,0:T(8,128)(2,1)}, bf16[144,2048]{1,0:T(8,128)(2,1)}, u32[]{:S(2)}, u32[]{:S(2)}) collective-permute-start(bf16[144,2048]{1,0:T(8,128)(2,1)} %collective-permute-done.59), channel_id=1, source_target_pairs={{0,8},{8,0},{16,24},{24,16},{1,9},{9,1},{17,25},{25,17},{2,10},{10... | collective-permute-start | bytes 1769480 | tf_op jit(solution)/shard_map/ppermute | solution.py:22
  (141 other events, 2054.4 us)
Sparse Core Ops, SparseCore 0:
  45.5 65.0 all-gather.5
  119.4 68.7 all-gather.3
  390.3 119.2 reduce-scatter.3
  525.6 119.2 reduce-scatter.5
  647.0 117.6 reduce-scatter.7
